TPU v7x, 128 devices: a whole 4x4x4 slice. The times are simulated.
128 devices in a mesh: dp: 4 (over x_hi, core), section: 4 (over z), tensor: 8 (over x_lo, y).
Axes of the slice: x: 4 (x_hi: 2, x_lo: 2; x = x_hi * 2 + x_lo), y: 4, z: 4, core: 2. Of those that a mesh axis runs over, the one named last changes fastest.
Arguments:
- embeds: bfloat16 [8, 128, 4096], P('dp', None, 'tensor'), may hold values from -6 to 6
- source: int32 [8], replicated, may hold values from 0 to 7, each once
- lengths: int32 [8], replicated, may hold values from 32 to 128, as said below
- bounds: int32 [8, 4], replicated, may hold values from 0 to 127, as said below
- targets: int32 [8, 4], replicated, may hold values from 0 to 127
- w_query: bfloat16 [4, 4096, 4096], P('section', None, 'tensor'), may hold values from -0.09375 to 0.09375
- w_key: bfloat16 [4, 4096, 1024], P('section', None, 'tensor'), may hold values from -0.09375 to 0.09375
- w_value: bfloat16 [4, 4096, 1024], P('section', None, 'tensor'), may hold values from -0.09375 to 0.09375
- w_out: bfloat16 [4, 4096, 4096], P('section', 'tensor'), may hold values from -0.09375 to 0.09375
- w_class: bfloat16 [4096, 128], P('tensor'), may hold values from -0.09375 to 0.09375
Outputs:
- grad_query: float32 [4, 4096, 4096], P('section', 'dp', 'tensor')
- grad_key: float32 [4, 4096, 1024], P('section', 'dp', 'tensor')
- grad_value: float32 [4, 4096, 1024], P('section', 'dp', 'tensor')
- grad_out: float32 [4, 4096, 4096], P('section', 'tensor', 'dp')
Inputs may be any that keep to these rules, and one draw needn't show every extreme that they name: `lengths`: a trace's length is at least 32; some trace has exactly 128 tokens. `bounds`: within a trace the step ends rise strictly and the last is its length minus one. `source`: each trace fills exactly one slot.
All inputs are finite; a program needn't handle non-finite values.
Results may differ from a plain program's by a relative error of at most 0.04.
Values may be sent and summed in bfloat16 or wider, within the bound.
No kernel may reach another device: no remote copies, remote signals or barrier semaphores. Data moves between devices by JAX's collectives and lax.ppermute only.
A program may use at most 320 MiB of HBM per device.

v0:
```python
import functools

import jax
import jax.numpy as jnp
from jax import lax
from jax.experimental import pallas as pl
from jax.experimental.pallas import tpu as pltpu
from jax.sharding import PartitionSpec as P

HEAD_DIM = 128
EPS = 1e-06
LOSS_SCALE = 16384.0
SCORE_SCALE = 1.0 / HEAD_DIM**0.5
F32 = jnp.float32
BF16 = jnp.bfloat16
VMEM_LIMIT = 16 * 1024 * 1024


def dot(a, b):
    return jnp.dot(a, b, preferred_element_type=F32)


def dot_nt(a, b):
    return lax.dot_general(a, b, (((1,), (1,)), ((), ())), preferred_element_type=F32)


def dot_tn(a, b):
    return lax.dot_general(a, b, (((0,), (0,)), ((), ())), preferred_element_type=F32)


def in_vmem():
    return pl.BlockSpec(memory_space=pltpu.VMEM)


def in_smem():
    return pl.BlockSpec(memory_space=pltpu.SMEM)


def anywhere():
    return pl.BlockSpec(memory_space=pl.ANY)


def kernel_params(limit):
    return pltpu.CompilerParams(vmem_limit_bytes=limit)


def heads_down(x, heads):
    return jnp.concatenate([x[:, n * HEAD_DIM : (n + 1) * HEAD_DIM] for n in range(heads)], axis=0)


def heads_across(x, heads):
    rows = x.shape[0] // heads
    return jnp.concatenate([x[n * rows : (n + 1) * rows] for n in range(heads)], axis=1)


def place_ends(ends_ref, block, rows, nstep):
    ends_ref[pl.ds(block * nstep, nstep), :] = rows[:nstep]


def forward_kernel(mode, nstep, len_ref, x_ref, wq_ref, wk_ref, wv_ref, wo_ref, *rest):
    if mode == "all":
        part_ref, h_ref, scale_ref, pack_ref, o_ref = rest
    else:
        pick_ref, part_ref, h_ref, scale_ref, pack_ref, o_ref, ends_ref = rest
    nblk, rows, dsh = x_ref.shape
    qh = wq_ref.shape[1] // HEAD_DIM
    sq = jnp.zeros((rows, 1), F32)
    for j in range(nblk):
        xf = x_ref[j].astype(F32)
        sq = sq + jnp.sum(xf * xf, axis=1, keepdims=True)
    scale = lax.rsqrt(sq / (nblk * dsh) + EPS)
    scale_ref[...] = jnp.broadcast_to(scale, scale_ref.shape)
    q = jnp.zeros((rows, wq_ref.shape[1]), F32)
    k = jnp.zeros((rows, HEAD_DIM), F32)
    v = jnp.zeros((rows, HEAD_DIM), F32)
    for j in range(nblk):
        h = (x_ref[j].astype(F32) * scale).astype(BF16)
        h_ref[j] = h
        at = pl.ds(j * dsh, dsh)
        q = q + dot(h, wq_ref[at, :])
        k = k + dot(h, wk_ref[at, :])
        v = v + dot(h, wv_ref[at, :])
    k = k.astype(BF16)
    v = v.astype(BF16)
    q = heads_down(q.astype(BF16), qh)
    top = qh * rows
    pack_ref[:top, :] = q
    pack_ref[pl.ds(2 * top, rows), :] = k
    pack_ref[pl.ds(2 * top + rows, rows), :] = v
    posq = lax.broadcasted_iota(jnp.int32, (rows, rows), 0)
    posk = lax.broadcasted_iota(jnp.int32, (rows, rows), 1)
    keep = ((posk <= posq) & (posk < len_ref[0])).astype(F32)
    expo = jnp.exp(dot_nt(q, k) * SCORE_SCALE) * jnp.concatenate([keep] * qh, axis=0)
    weights = (expo / jnp.sum(expo, axis=1, keepdims=True)).astype(BF16)
    pack_ref[pl.ds(top, top), :] = weights
    o_ref[...] = heads_across(dot(weights, v).astype(BF16), qh)
    o = o_ref[...]
    if mode != "all":
        picked = dot(pick_ref[...], o).astype(BF16)
        o = picked if mode == "ends" else jnp.concatenate([o, picked], axis=0)
    for j in range(nblk):
        part = dot(o, wo_ref[:, pl.ds(j * dsh, dsh)])
        if mode != "ends":
            part_ref[j, :rows] = part[:rows].astype(BF16)
        if mode != "all":
            place_ends(ends_ref, j, part[-pick_ref.shape[0] :], nstep)
    if mode == "ends":
        part_ref[...] = ends_ref[...].astype(BF16)
    elif mode == "both":
        for j in range(nblk):
            part_ref[j, rows:] = ends_ref[...].astype(BF16)


def forward(length, x, weights, mode="all", pick=None, nstep=0):
    nblk, rows, dsh = x.shape
    qcol = weights[0].shape[1]
    packed = 2 * qcol // HEAD_DIM * rows + 2 * rows
    nend = nblk * nstep
    part = {"all": x.shape, "both": (nblk, rows + nend, dsh), "ends": (nend, dsh)}[mode]
    outs = [(part, BF16), (x.shape, BF16)]
    outs += [((rows, HEAD_DIM), F32), ((packed, HEAD_DIM), BF16), ((rows, qcol), BF16)]
    more = [] if mode == "all" else [pick]
    out = pl.pallas_call(
        functools.partial(forward_kernel, mode, nstep),
        out_shape=tuple(jax.ShapeDtypeStruct(*one) for one in outs),
        in_specs=[in_smem()] + [in_vmem()] * (5 + len(more)),
        out_specs=tuple([in_vmem()] * 5),
        scratch_shapes=[pltpu.VMEM((nend, dsh), F32)] if more else [],
        compiler_params=kernel_params(VMEM_LIMIT),
        cost_estimate=pl.CostEstimate(
            flops=2 * rows * nblk * dsh * (2 * qcol + 2 * HEAD_DIM),
            bytes_accessed=4 * nblk * dsh * (qcol + HEAD_DIM),
            transcendentals=rows * rows * qcol // HEAD_DIM,
        ),
        name="forward_layer",
    )(length, x, *weights, *more)
    return dict(zip(("part", "h", "scale", "pack", "o"), out))


def step_end_kernel(nstep, factor_ref, got_ref, x_ref, pick_ref, class_ref, hot_ref, out_ref, sum_ref, row_ref):
    nblk, rows, dsh = x_ref.shape
    width = nblk * dsh
    nend = nblk * nstep
    parts = jnp.zeros((nend, dsh), F32)
    for j in range(nblk):
        parts = parts + got_ref[j, rows:].astype(F32)
    sum_ref[...] = parts
    npad = pick_ref.shape[0]
    row_ref[...] = jnp.zeros(row_ref.shape, F32)
    zeta = jnp.zeros((npad, class_ref.shape[1]), F32)
    sumsq = jnp.zeros((npad, 1), F32)
    for j in range(nblk):
        row_ref[j, :nstep] = sum_ref[pl.ds(j * nstep, nstep), :]
        full = (dot(pick_ref[...], x_ref[j]) + row_ref[j]).astype(BF16)
        ff = full.astype(F32)
        row_ref[j] = ff
        zeta = zeta + dot(full, class_ref[pl.ds(j * dsh, dsh), :])
        sumsq = sumsq + jnp.sum(ff * ff, axis=1, keepdims=True)
    rstd = lax.rsqrt(sumsq / width + EPS)
    expo = jnp.exp(zeta * rstd)
    prob = expo / jnp.sum(expo, axis=1, keepdims=True)
    dlog = factor_ref[0] * (prob - hot_ref[...])
    dzeta = dlog * rstd
    dmean = jnp.sum(dlog * zeta, axis=1, keepdims=True) * -0.5 * rstd * rstd * rstd
    high = dzeta.astype(BF16)
    mid = (dzeta - high.astype(F32)).astype(BF16)
    low = (dzeta - high.astype(F32) - mid.astype(F32)).astype(BF16)
    terms = jnp.concatenate([high, mid, low], axis=0)
    for j in range(nblk):
        head = class_ref[pl.ds(j * dsh, dsh), :]
        back = dot_nt(terms, head)
        back = back[:npad] + (back[npad : 2 * npad] + back[2 * npad :])
        back = (back + dmean * 2.0 * row_ref[j] / width).astype(BF16)
        out_ref[j] = dot_tn(pick_ref[...], back).astype(BF16)


def step_end_grad(factor, got, x, pick, w_class, hot, nstep):
    nblk, rows, dsh = x.shape
    return pl.pallas_call(
        functools.partial(step_end_kernel, nstep),
        out_shape=jax.ShapeDtypeStruct(x.shape, BF16),
        in_specs=[in_smem()] + [in_vmem()] * 5,
        out_specs=in_vmem(),
        scratch_shapes=[
            pltpu.VMEM((nblk * nstep, dsh), F32),
            pltpu.VMEM((nblk, pick.shape[0], dsh), F32),
        ],
        compiler_params=kernel_params(VMEM_LIMIT),
        cost_estimate=pl.CostEstimate(
            flops=16 * rows * nblk * dsh * pick.shape[0], bytes_accessed=4 * rows * nblk * dsh,
            transcendentals=0,
        ),
        name="step_end_grad",
    )(factor, got, x, pick, w_class, hot)


def backward_kernel(
    with_input, with_ends, nheld, flag_ref, g_ref, pack0_ref, pack1_ref, h0_ref, h1_ref,
    scale0_ref, scale1_ref, wq_ref, wk_ref, wv_ref, wo_ref, *rest
):
    rest = rest[nheld:]
    if with_ends:
        ends_ref, rest = rest[0], rest[1:]
    if with_input:
        d_ref, dx_ref, pack_ref, keep_sems, h_ref, scale_ref, dh_ref = rest
    else:
        d_ref, pack_ref, keep_sems = rest
    nblk, rows, dsh = g_ref.shape
    qcol = wq_ref.shape[1]
    qh = qcol // HEAD_DIM
    top = qh * rows
    pairs = [(pack0_ref, pack1_ref, pack_ref)]
    if with_input:
        pairs += [(h0_ref, h1_ref, h_ref), (scale0_ref, scale1_ref, scale_ref)]
    for at, (one, two, to) in enumerate(pairs):

        @pl.when(flag_ref[0] == 0)
        def _(one=one, to=to, at=at):
            pltpu.make_async_copy(one, to, keep_sems.at[at]).start()

        @pl.when(flag_ref[0] != 0)
        def _(two=two, to=to, at=at):
            pltpu.make_async_copy(two, to, keep_sems.at[at]).start()

    do = jnp.zeros((rows, qcol), F32)
    for j in range(nblk):
        do = do + dot_nt(g_ref[j], wo_ref[:, pl.ds(j * dsh, dsh)])
    do = do.astype(BF16)
    pltpu.make_async_copy(pack0_ref, pack_ref, keep_sems.at[0]).wait()
    k = pack_ref[pl.ds(2 * top, rows), :]
    v = pack_ref[pl.ds(2 * top + rows, rows), :]
    do = heads_down(do, qh)
    weights = pack_ref[pl.ds(top, top), :]
    wf = weights.astype(F32)
    dw = dot_nt(do, v)
    ds = wf * (dw - jnp.sum(dw * wf, axis=1, keepdims=True)) * SCORE_SCALE
    ds = ds.astype(BF16)
    dk = dot_tn(ds, pack_ref[:top, :])
    dv = dot_tn(weights, do)
    d_ref[:, :qcol] = heads_across(dot(ds, k).astype(BF16), qh)
    d_ref[:, qcol : qcol + HEAD_DIM] = dk.astype(BF16)
    d_ref[:, qcol + HEAD_DIM :] = dv.astype(BF16)
    if not with_input:
        return
    pltpu.make_async_copy(h0_ref, h_ref, keep_sems.at[1]).wait()
    pltpu.make_async_copy(scale0_ref, scale_ref, keep_sems.at[2]).wait()
    dq = d_ref[:, :qcol]
    dk = dk.astype(BF16)
    dv = dv.astype(BF16)
    inner = jnp.zeros((rows, 1), F32)
    for j in range(nblk):
        at = pl.ds(j * dsh, dsh)
        dh = dot_nt(dq, wq_ref[at, :]) + dot_nt(dk, wk_ref[at, :]) + dot_nt(dv, wv_ref[at, :])
        dh_ref[j] = dh
        inner = inner + jnp.sum(dh * h_ref[j].astype(F32), axis=1, keepdims=True)
    inner = inner / (nblk * dsh)
    scale = scale_ref[:, :1]
    for j in range(nblk):
        dx_ref[j, :rows] = (scale * (dh_ref[j] - h_ref[j].astype(F32) * inner)).astype(BF16)
        if with_ends:
            dx_ref[j, rows:] = ends_ref[...]


def backward(flag, g, one, two, weights, with_input, ends=(), held=()):
    nblk, rows, dsh = g.shape
    wq, wk, wv, wo = weights
    qcol = wq.shape[1]
    out_shape = [jax.ShapeDtypeStruct((rows, qcol + 2 * HEAD_DIM), BF16)]
    scratch = [pltpu.VMEM(one["pack"].shape, BF16), pltpu.SemaphoreType.DMA((3,))]
    if with_input:
        below = sum(x.shape[0] for x in ends)
        out_shape.append(jax.ShapeDtypeStruct((nblk, rows + below, dsh), BF16))
        scratch += [
            pltpu.VMEM(g.shape, BF16),
            pltpu.VMEM(one["scale"].shape, F32),
            pltpu.VMEM(g.shape, F32),
        ]
    return pl.pallas_call(
        functools.partial(backward_kernel, with_input, bool(ends), len(held)),
        out_shape=tuple(out_shape),
        in_specs=[in_smem(), in_vmem()]
        + [anywhere()] * 6
        + [in_vmem()] * 4
        + [anywhere()] * len(held)
        + [in_vmem()] * len(ends),
        out_specs=tuple([in_vmem()] * len(out_shape)),
        scratch_shapes=scratch,
        compiler_params=kernel_params(VMEM_LIMIT),
        cost_estimate=pl.CostEstimate(
            flops=2 * rows * nblk * dsh * (2 * qcol + 2 * HEAD_DIM) if with_input else 1,
            bytes_accessed=4 * nblk * dsh * (qcol + HEAD_DIM) if with_input else 1,
            transcendentals=0,
        ),
        name="backward_layer" if with_input else "backward_heads",
    )(
        flag, g, one["pack"], two["pack"], one["h"], two["h"],
        one["scale"], two["scale"], wq, wk, wv, wo, *held, *ends,
    )


def weight_grad_kernel(wide_first, runs, nnarrow, splits, quarter_ref, *refs):
    nwide, nout = sum(runs), len(splits)
    wides, narrows = refs[:nwide], refs[nwide : nwide + nnarrow]
    given, outs = refs[nwide + nnarrow : -nout - 2], refs[-nout - 2 : -2]
    wide_all, narrow_all = refs[-2:]
    quarter = quarter_ref[0]
    at = 0
    for i, n in enumerate(runs):
        run = wides[at : at + n]
        at += n
        rows, dsh = run[0].shape[1:]
        here = pl.ds(i * rows, rows)
        if n == 1:
            half = run[0].shape[0] // 2
            for b in range(half):
                wide_all[here, pl.ds(b * dsh, dsh)] = run[0][quarter * half + b]
        for which, piece in enumerate(run if n > 1 else ()):

            @pl.when(quarter == which)
            def _(piece=piece):
                for b in range(piece.shape[0]):
                    wide_all[here, pl.ds(b * dsh, dsh)] = piece[b]

    rows = narrows[0].shape[0]
    for i, piece in enumerate(narrows):
        narrow_all[pl.ds(i * rows, rows), :] = piece[...]
    for c in range(outs[0].shape[0] // 256):
        cols = pl.ds(c * 256, 256)
        if wide_first:
            got = dot_tn(wide_all[:, cols], narrow_all[...])
        else:
            got = dot_tn(narrow_all[:, cols], wide_all[...])
        for more in given:
            got = got + more[cols, :].astype(F32)
        for out_ref, (start, stop) in zip(outs, splits):
            out_ref[cols, :] = got[:, start:stop].astype(out_ref.dtype)


def weight_grad(quarter, wide, narrow, wide_first, widths, dtype, given=()):
    rows, cols = narrow[0].shape
    dsh = wide[0][0].shape[2]
    width = sum(x.shape[0] for x in wide[0]) * dsh // 2
    height = width if wide_first else cols
    total = len(narrow) * rows
    flat = [x for run in wide for x in run]
    splits = [(sum(widths[:i]), sum(widths[: i + 1])) for i in range(len(widths))]
    runs = tuple(len(run) for run in wide)
    return pl.pallas_call(
        functools.partial(weight_grad_kernel, wide_first, runs, len(narrow), tuple(splits)),
        out_shape=tuple(jax.ShapeDtypeStruct((height, w), dtype) for w in widths),
        in_specs=[in_smem()] + [in_vmem()] * (len(flat) + len(narrow) + len(given)),
        out_specs=tuple([in_vmem()] * len(widths)),
        scratch_shapes=[pltpu.VMEM((total, width), BF16), pltpu.VMEM((total, cols), BF16)],
        compiler_params=kernel_params(VMEM_LIMIT),
        cost_estimate=pl.CostEstimate(flops=1, bytes_accessed=1, transcendentals=0),
        name="weight_grad",
    )(quarter, *flat, *narrow, *given)


def passed_along(x, axis, by):
    peers = lax.axis_size(axis)
    pairs = [(i, i + by) for i in range(peers) if 0 <= i + by < peers]
    return lax.ppermute(x, axis, pairs)


def swapped(x, axis, mask):
    return lax.ppermute(x, axis, [(i, i ^ mask) for i in range(lax.axis_size(axis))])


def mirrored(x, mask):
    ndp, peers = lax.axis_size("dp"), lax.axis_size("tensor")
    to = lambda p, r: (p ^ mask) * peers + (r + peers // 2) % peers
    pairs = [(p * peers + r, to(p, r)) for p in range(ndp) for r in range(peers)]
    return lax.ppermute(x, ("dp", "tensor"), pairs)


def held_back(x):
    return lax.ppermute(x[:16, :128], "dp", [(i, i + 1) for i in range(0, lax.axis_size("dp"), 2)])


def exchange(blocks):
    return lax.all_to_all(blocks, "tensor", split_axis=0, concat_axis=0, tiled=True)


def gathered(cur):
    return exchange(jnp.broadcast_to(cur[None], (lax.axis_size("tensor"),) + cur.shape))


def by_section(masks, choices):
    out = choices[-1]
    for mask, choice in zip(masks, choices[:-1]):
        out = jnp.where(mask, choice, out)
    return out


def after(x, *marks):
    return lax.optimization_barrier((x,) + marks)[0]


def together(*xs):
    return lax.optimization_barrier(xs)


def on_device(embeds, source, lengths, bounds, targets, w_query, w_key, w_value, w_out, w_class):
    nst = lax.axis_size("section")
    peers = lax.axis_size("tensor")
    rep = lax.axis_index("dp")
    section_at = lax.axis_index("section")
    tensor_at = lax.axis_index("tensor")
    ntr, width, dsh = embeds.shape
    weights = (w_query[0], w_key[0], w_value[0], w_out[0])
    w_class = gathered(w_class).reshape(peers * w_class.shape[0], w_class.shape[1])

    hi, core = rep // 2, rep % 2
    slots = source.reshape(2, 2, ntr) - rep * ntr

    def mine_for(col):
        owner = lax.dynamic_slice_in_dim(slots, col, 1, axis=1)[:, 0]
        out = jnp.zeros((2, ntr, width, dsh), BF16)
        for n in range(ntr):
            out = jnp.where((owner == n)[:, :, None, None], embeds[n][None, None], out)
        return out

    both = mine_for(core) + swapped(mine_for(1 - core), "dp", 1)
    own = lax.dynamic_slice_in_dim(both, hi, 1, axis=0)[0]
    away = lax.dynamic_slice_in_dim(both, 1 - hi, 1, axis=0)[0]
    taken_here = own + swapped(away, "dp", 2)
    source, lengths, bounds, targets, taken_here = together(
        source, lengths, bounds, targets, taken_here
    )
    wanted = lax.dynamic_slice_in_dim(source, rep * ntr, ntr)
    lens = lengths[wanted]
    bnd = bounds[wanted]
    tgt = targets[wanted]
    nstep = bnd.shape[1]
    factor = (LOSS_SCALE / jnp.sum(lens).astype(F32)).reshape(1)

    def one_hot(ids, size):
        hot = ids[:, None] == jnp.arange(size, dtype=jnp.int32)[None, :]
        return jnp.concatenate([hot, jnp.zeros((16 - nstep, size), bool)], axis=0)

    picks = [one_hot(bnd[j], width).astype(BF16) for j in range(ntr)]
    hots = [one_hot(tgt[j], w_class.shape[1]).astype(F32) for j in range(ntr)]
    spans = [jnp.where(section_at == n, lens[0], lens[1]).reshape(1) for n in range(nst + 1)]
    flags = [(section_at == s).astype(jnp.int32).reshape(1) for s in range(nst)]
    masks = [section_at == s for s in range(nst)]
    half = peers // 2
    mine_at = (hi * half).astype(jnp.uint32)
    away_at = [((1 - hi) * half + n * half // 2).astype(jnp.uint32) for n in range(2)]
    block_at = tensor_at.astype(jnp.uint32)
    ours = core.astype(jnp.int32).reshape(1)
    theirs = 1 - ours

    def sum_of(got):
        return jnp.sum(got[:, :width].astype(F32), axis=0)

    kept = []
    arriving = None
    for turn in range(nst):
        cur = taken_here[turn] if turn < ntr else jnp.zeros((width, dsh), BF16)
        if turn == 0:
            cur, factor, picks, hots, spans, flags, masks, mine_at, away_at, block_at, ours, theirs, w_class = together(
                cur, factor, picks, hots, spans, flags, masks, mine_at, away_at, block_at, ours, theirs, w_class
            )
        if arriving is not None:
            cur, arriving = together(cur, arriving)
            cur = jnp.where(masks[0], cur, arriving)
        x = gathered(cur)
        if turn == nst - 1:
            now = forward(spans[turn], x, weights, "both", picks[0], nstep)
        else:
            now = forward(spans[turn], x, weights)
        kept.append(now)
        blocks = now["part"]
        got = exchange(blocks)
        arriving = (cur.astype(F32) + sum_of(got)).astype(BF16)
        leaving = arriving
        arriving = passed_along(arriving, "section", 1)

    def end_cotangent(which, got, x):
        return step_end_grad(factor, got, x, picks[which], w_class, hots[which], nstep)

    def own_block(blocks):
        return lax.dynamic_slice_in_dim(blocks, block_at, 1, axis=0)[0]

    def chosen(choices, at=None, count=None):
        if at is None:
            return by_section(masks, choices)
        return by_section(
            masks, [lax.dynamic_slice_in_dim(x, at, count, axis=0) for x in choices]
        )

    def not_before(choices, mark):
        return [after(x, mark) for x in choices]

    seen = lambda name, which: [kept[s + which][name] for s in range(nst)]
    back = lambda n, which: [taken[2 * nst - 1 - s + which][n] for s in range(nst)]

    pieces = {}

    def send_blocks(name, choices, n):
        pieces[f"{name}.{n}"] = mirrored(chosen(choices, away_at[n], half // 2), 2)

    def send_half(name, choices):
        pieces[name] = mirrored(chosen(choices, away_at[0], half), 2)

    def send_whole(name, choices):
        pieces[name] = swapped(chosen(choices), "dp", 2)

    taken = {}
    g_top = end_cotangent(0, got, x)
    grad = own_block(g_top)
    send_blocks("h0", not_before(seen("h", 0), leaving), 0)
    send_whole("o0", not_before(seen("o", 0), leaving))
    arriving, g_top, grad, pieces = together(arriving, g_top, grad, pieces)
    x = gathered(arriving)
    now = forward(spans[nst], x, weights, "ends", picks[1], nstep)
    d, dx = backward(
        jnp.zeros((1,), jnp.int32), g_top, kept[-1], kept[-1], weights, True, (now["part"],)
    )
    taken[nst] = (d, g_top)
    kept.append(now)
    got = exchange(dx)

    for turn in range(nst + 1, 2 * nst + 1):
        grad = (grad.astype(F32) + sum_of(got)).astype(BF16)
        leaving = grad
        if turn == nst + 1:
            g_top = end_cotangent(1, got, x)
            send_blocks("h0", not_before(seen("h", 0), grad), 1)
            send_whole("o1", not_before(seen("o", 1), grad))
        elif turn < 2 * nst:
            n = turn - nst - 2
            send_blocks("h1", not_before(seen("h", 1), grad), n)
        else:
            send_half("g0", not_before(back(1, 0), grad))
            send_whole("d0", not_before(back(0, 0), grad))
        held = [held_back(leaving)] if turn == nst + 1 else []
        grad, pieces, held = together(passed_along(grad, "section", -1), pieces, held)
        if turn == nst + 1:
            grad = jnp.where(masks[nst - 1], own_block(g_top), grad)
        g = gathered(grad)
        late = 2 * nst + 1 - turn
        early = max(late - 2, 0)
        flag = flags[late - 1]
        if turn < 2 * nst:
            d, dx = backward(flag, g, kept[early], kept[late], weights, True, (), held)
            taken[turn] = (d, g)
            got = exchange(dx)
        else:
            taken[turn] = (None, g)
            send_half("g1", back(1, 1))
            (d,) = backward(flag, g, kept[early], kept[late], weights, False)
            taken[turn] = (d, g)
            send_whole("d1", back(0, 1))

    def wide(name, choices):
        runs = []
        for w in range(ntr):
            runs.append((chosen(not_before(choices(w), g), mine_at, half),))
            names = (f"{name}{w}",) if name == "g" else (f"{name}{w}.0", f"{name}{w}.1")
            runs.append(tuple(pieces[n] for n in names))
        return runs

    def narrow(name, choices):
        out = []
        for w in range(ntr):
            out += [chosen(not_before(choices(w), g)), pieces[f"{name}{w}"]]
        return out

    qcol = weights[0].shape[1]
    all_o = (wide("g", lambda w: back(1, w)), narrow("o", lambda w: seen("o", w)), False)
    all_d = (wide("h", lambda w: seen("h", w)), narrow("d", lambda w: back(0, w)), True)
    cols_o, cols_d = (half // 2 * dsh,), (qcol, HEAD_DIM, HEAD_DIM)
    (give_o,) = weight_grad(theirs, *all_o, cols_o, BF16)
    given_o = swapped(give_o, "dp", 1)
    (give_d,) = weight_grad(theirs, *all_d, (sum(cols_d),), BF16)
    given_d = swapped(give_d, "dp", 1)
    (grad_o,) = weight_grad(ours, *all_o, cols_o, F32, (given_o,))
    grad_q, grad_k, grad_v = weight_grad(ours, *all_d, cols_d, F32, (given_d,))
    return (grad_q[None], grad_k[None], grad_v[None], grad_o[None])


def solution(mesh):
    placed = (
        P("dp", None, "tensor"),
        P(),
        P(),
        P(),
        P(),
        P("section", None, "tensor"),
        P("section", None, "tensor"),
        P("section", None, "tensor"),
        P("section", "tensor", None),
        P("tensor", None),
    )
    return jax.shard_map(
        on_device,
        mesh=mesh,
        in_specs=placed,
        out_specs=(
            P("section", "dp", "tensor"),
            P("section", "dp", "tensor"),
            P("section", "dp", "tensor"),
            P("section", "tensor", "dp"),
        ),
        check_vma=False,
    )
```

profile of v0, /device:TPU:1, one launch (start us, length us, event | category | flops | bytes accessed | tf_op | source)
XLA Modules:
  0.0 423.6 jit_solution(13323900372384934499)
XLA Ops:
  5.9 2.9 collective-permute-start.1
  9.9 4.2 all-to-all-start
  29.1 17.1 %all_to_all.90.x_ref = bf16[8,128,512]{2,1,0:T(8,128)(2,1)S(1)} all-to-all(bf16[8,128,512]{2,1,0:T(8,128)(2,1)S(1)} %broadcast_in_dim.141), channel_id=1, replica_groups=mesh['dp'=4,'section'=4,'tensor'=8] {'tensor'}, dimensions={0} | all-to-all | bytes 2097152 | tf_op jit(solution)/shard_map/all_to_all | solution.py:382
  46.3 2.2 copy-done.2
  48.4 2.2 copy-done.4
  50.6 2.5 forward_layer.5
  53.2 16.2 %all_to_all.91 = bf16[8,128,512]{2,1,0:T(8,128)(2,1)S(1)} all-to-all(bf16[8,128,512]{2,1,0:T(8,128)(2,1)S(1)} %get-tuple-element.173), channel_id=1, replica_groups=mesh['dp'=4,'section'=4,'tensor'=8] {'tensor'}, dimensions={0} | all-to-all | bytes 2097152 | tf_op jit(solution)/shard_map/all_to_all | solution.py:382
  69.6 3.8 collective-permute-start.2
  75.5 13.4 %all_to_all.92.x_ref = bf16[8,128,512]{2,1,0:T(8,128)(2,1)S(1)} all-to-all(bf16[8,128,512]{2,1,0:T(8,128)(2,1)S(1)} %broadcast_in_dim.142), channel_id=1, replica_groups=mesh['dp'=4,'section'=4,'tensor'=8] {'tensor'}, dimensions={0} | all-to-all | bytes 2097152 | tf_op jit(solution)/shard_map/all_to_all | solution.py:382
  88.9 2.5 forward_layer.6
  91.4 13.8 %all_to_all.93 = bf16[8,128,512]{2,1,0:T(8,128)(2,1)S(1)} all-to-all(bf16[8,128,512]{2,1,0:T(8,128)(2,1)S(1)} %get-tuple-element.177), channel_id=1, replica_groups=mesh['dp'=4,'section'=4,'tensor'=8] {'tensor'}, dimensions={0} | all-to-all | bytes 2097152 | tf_op jit(solution)/shard_map/all_to_all | solution.py:382
  105.4 3.6 collective-permute-start.3
  111.1 12.7 %all_to_all.94.x_ref = bf16[8,128,512]{2,1,0:T(8,128)(2,1)S(1)} all-to-all(bf16[8,128,512]{2,1,0:T(8,128)(2,1)S(1)} %broadcast_in_dim.143), channel_id=1, replica_groups=mesh['dp'=4,'section'=4,'tensor'=8] {'tensor'}, dimensions={0} | all-to-all | bytes 2097152 | tf_op jit(solution)/shard_map/all_to_all | solution.py:382
  123.8 2.5 forward_layer.7
  126.4 12.7 %all_to_all.95 = bf16[8,128,512]{2,1,0:T(8,128)(2,1)S(1)} all-to-all(bf16[8,128,512]{2,1,0:T(8,128)(2,1)S(1)} %get-tuple-element.183), channel_id=1, replica_groups=mesh['dp'=4,'section'=4,'tensor'=8] {'tensor'}, dimensions={0} | all-to-all | bytes 2097152 | tf_op jit(solution)/shard_map/all_to_all | solution.py:382
  139.3 3.8 collective-permute-start.4
  145.1 12.9 %all_to_all.96.x_ref = bf16[8,128,512]{2,1,0:T(8,128)(2,1)S(1)} all-to-all(bf16[8,128,512]{2,1,0:T(8,128)(2,1)S(1)} %broadcast_in_dim.144), channel_id=1, replica_groups=mesh['dp'=4,'section'=4,'tensor'=8] {'tensor'}, dimensions={0} | all-to-all | bytes 2097152 | tf_op jit(solution)/shard_map/all_to_all | solution.py:382
  158.0 2.7 forward_layer.8
  160.7 15.9 %all_to_all.97.got_ref = bf16[8,160,512]{2,1,0:T(8,128)(2,1)S(1)} all-to-all(bf16[8,160,512]{2,1,0:T(8,128)(2,1)S(1)} %get-tuple-element.188), channel_id=1, replica_groups=mesh['dp'=4,'section'=4,'tensor'=8] {'tensor'}, dimensions={0} | all-to-all | bytes 2621440 | tf_op jit(solution)/shard_map/all_to_all | solution.py:382
  179.4 4.1 collective-permute-start.5
  183.5 2.7 step_end_grad.2.g_ref
  186.4 14.0 %all_to_all.98.x_ref = bf16[8,128,512]{2,1,0:T(8,128)(2,1)S(1)} all-to-all(bf16[8,128,512]{2,1,0:T(8,128)(2,1)S(1)} %broadcast_in_dim.145), channel_id=1, replica_groups=mesh['dp'=4,'section'=4,'tensor'=8] {'tensor'}, dimensions={0} | all-to-all | bytes 2097152 | tf_op jit(solution)/shard_map/all_to_all | solution.py:382
  200.4 2.6 forward_layer.9
  203.0 4.8 %backward_layer.4 = (bf16[128,768]{1,0:T(8,128)(2,1)S(1)}, bf16[8,160,512]{2,1,0:T(8,128)(2,1)S(1)}) custom-call(s32[1]{0:T(128)} %constant.63.clone.1.flag_ref, bf16[8,128,512]{2,1,0:T(8,128)(2,1)S(1)} %step_end_grad.2.g_ref, bf16[1280,128]{1,0:T(8,128)(2,1)S(1)} %get-tuple-element.210.pack0_ref.pack1_ref, ...), custom_call_target="tpu_custom_call" | custom-call | flops 1342177280 | bytes 10485760 | tf_op jit(solution)/shard_map/backward_layer/pallas_call | solution.py:278
  207.8 14.6 %all_to_all.99.got_ref = bf16[8,160,512]{2,1,0:T(8,128)(2,1)S(1)} all-to-all(bf16[8,160,512]{2,1,0:T(8,128)(2,1)S(1)} %get-tuple-element.216), channel_id=1, replica_groups=mesh['dp'=4,'section'=4,'tensor'=8] {'tensor'}, dimensions={0} | all-to-all | bytes 2621440 | tf_op jit(solution)/shard_map/all_to_all | solution.py:382
  227.9 2.7 step_end_grad.3
  230.6 16.0 %collective-permute-done.11.rest_0_ = bf16[16,128]{1,0:T(8,128)(2,1)S(1)} collective-permute-done((bf16[16,128]{1,0:T(8,128)(2,1)S(1)}, bf16[16,128]{1,0:T(8,128)(2,1)S(1)}, u32[]{:S(2)}, u32[]{:S(2)}) %collective-permute-start.11) | collective-permute-done | bytes 4128 | tf_op jit(solution)/shard_map/ppermute | solution.py:378
  246.7 13.4 %all_to_all.100.g_ref = bf16[8,128,512]{2,1,0:T(8,128)(2,1)S(1)} all-to-all(bf16[8,128,512]{2,1,0:T(8,128)(2,1)S(1)} %broadcast_in_dim.146), channel_id=1, replica_groups=mesh['dp'=4,'section'=4,'tensor'=8] {'tensor'}, dimensions={0} | all-to-all | bytes 2097152 | tf_op jit(solution)/shard_map/all_to_all | solution.py:382
  260.2 5.0 %backward_layer.5 = (bf16[128,768]{1,0:T(8,128)(2,1)S(1)}, bf16[8,128,512]{2,1,0:T(8,128)(2,1)S(1)}) custom-call(s32[1]{0:T(128)} %bitcast.20.flag_ref, bf16[8,128,512]{2,1,0:T(8,128)(2,1)S(1)} %all_to_all.100.g_ref, bf16[1280,128]{1,0:T(8,128)(2,1)S(1)} %get-tuple-element.233.pack0_ref.pack1_ref, bf16[1280,128]{1,0:T(8,128)(2,1)S(1)} %get-tuple-element.234.pack1_ref, ...), custom_call_target="tpu_custom_call" | custom-call | flops 1342177280 | bytes 10485760 | tf_op jit(solution)/shard_map/backward_layer/pallas_call | solution.py:278
  265.2 13.5 %all_to_all.101 = bf16[8,128,512]{2,1,0:T(8,128)(2,1)S(1)} all-to-all(bf16[8,128,512]{2,1,0:T(8,128)(2,1)S(1)} %get-tuple-element.239), channel_id=1, replica_groups=mesh['dp'=4,'section'=4,'tensor'=8] {'tensor'}, dimensions={0} | all-to-all | bytes 2097152 | tf_op jit(solution)/shard_map/all_to_all | solution.py:382
  281.9 5.4 %collective-permute-done.12 = bf16[128,512]{1,0:T(8,128)(2,1)S(1)} collective-permute-done((bf16[128,512]{1,0:T(8,128)(2,1)S(1)}, bf16[128,512]{1,0:T(8,128)(2,1)S(1)}, u32[]{:S(2)}, u32[]{:S(2)}) %collective-permute-start.12) | collective-permute-done | bytes 131104 | tf_op jit(solution)/shard_map/ppermute | solution.py:363
  287.4 12.7 %all_to_all.102.g_ref = bf16[8,128,512]{2,1,0:T(8,128)(2,1)S(1)} all-to-all(bf16[8,128,512]{2,1,0:T(8,128)(2,1)S(1)} %broadcast_in_dim.147), channel_id=1, replica_groups=mesh['dp'=4,'section'=4,'tensor'=8] {'tensor'}, dimensions={0} | all-to-all | bytes 2097152 | tf_op jit(solution)/shard_map/all_to_all | solution.py:382
  300.2 4.8 %backward_layer.6 = (bf16[128,768]{1,0:T(8,128)(2,1)S(1)}, bf16[8,128,512]{2,1,0:T(8,128)(2,1)S(1)}) custom-call(s32[1]{0:T(128)} %bitcast.19.flag_ref, bf16[8,128,512]{2,1,0:T(8,128)(2,1)S(1)} %all_to_all.102.g_ref, bf16[1280,128]{1,0:T(8,128)(2,1)S(1)} %get-tuple-element.250.pack0_ref.pack1_ref, ...), custom_call_target="tpu_custom_call" | custom-call | flops 1342177280 | bytes 10485760 | tf_op jit(solution)/shard_map/backward_layer/pallas_call | solution.py:278
  305.0 12.7 %all_to_all.103 = bf16[8,128,512]{2,1,0:T(8,128)(2,1)S(1)} all-to-all(bf16[8,128,512]{2,1,0:T(8,128)(2,1)S(1)} %get-tuple-element.252), channel_id=1, replica_groups=mesh['dp'=4,'section'=4,'tensor'=8] {'tensor'}, dimensions={0} | all-to-all | bytes 2097152 | tf_op jit(solution)/shard_map/all_to_all | solution.py:382
  320.4 8.3 %collective-permute-done.14 = bf16[128,512]{1,0:T(8,128)(2,1)S(1)} collective-permute-done((bf16[128,512]{1,0:T(8,128)(2,1)S(1)}, bf16[128,512]{1,0:T(8,128)(2,1)S(1)}, u32[]{:S(2)}, u32[]{:S(2)}) %collective-permute-start.14) | collective-permute-done | bytes 131104 | tf_op jit(solution)/shard_map/ppermute | solution.py:363
  328.8 12.7 %all_to_all.104.g_ref = bf16[8,128,512]{2,1,0:T(8,128)(2,1)S(1)} all-to-all(bf16[8,128,512]{2,1,0:T(8,128)(2,1)S(1)} %broadcast_in_dim.148), channel_id=1, replica_groups=mesh['dp'=4,'section'=4,'tensor'=8] {'tensor'}, dimensions={0} | all-to-all | bytes 2097152 | tf_op jit(solution)/shard_map/all_to_all | solution.py:382
  341.5 4.8 %backward_layer.7 = (bf16[128,768]{1,0:T(8,128)(2,1)S(1)}, bf16[8,128,512]{2,1,0:T(8,128)(2,1)S(1)}) custom-call(s32[1]{0:T(128)} %bitcast.18.flag_ref, bf16[8,128,512]{2,1,0:T(8,128)(2,1)S(1)} %all_to_all.104.g_ref, bf16[1280,128]{1,0:T(8,128)(2,1)S(1)} %get-tuple-element.264.pack0_ref, bf16[1280,128]{1,0:T(8,128)(2,1)S(1)} %get-tuple-element.233.pack0_ref.pack1_ref, ...), custom_call_target="tpu_custom_call" | custom-call | flops 1342177280 | bytes 10485760 | tf_op jit(solution)/shard_map/backward_layer/pallas_call | solution.py:278
  346.3 12.7 %all_to_all.105 = bf16[8,128,512]{2,1,0:T(8,128)(2,1)S(1)} all-to-all(bf16[8,128,512]{2,1,0:T(8,128)(2,1)S(1)} %get-tuple-element.266), channel_id=1, replica_groups=mesh['dp'=4,'section'=4,'tensor'=8] {'tensor'}, dimensions={0} | all-to-all | bytes 2097152 | tf_op jit(solution)/shard_map/all_to_all | solution.py:382
  363.1 5.0 %collective-permute-done.16 = bf16[128,512]{1,0:T(8,128)(2,1)S(1)} collective-permute-done((bf16[128,512]{1,0:T(8,128)(2,1)S(1)}, bf16[128,512]{1,0:T(8,128)(2,1)S(1)}, u32[]{:S(2)}, u32[]{:S(2)}) %collective-permute-start.16) | collective-permute-done | bytes 131104 | tf_op jit(solution)/shard_map/ppermute | solution.py:363
  371.2 14.7 %all_to_all.106.g_ref = bf16[8,128,512]{2,1,0:T(8,128)(2,1)S(1)} all-to-all(bf16[8,128,512]{2,1,0:T(8,128)(2,1)S(1)} %broadcast_in_dim.149), channel_id=1, replica_groups=mesh['dp'=4,'section'=4,'tensor'=8] {'tensor'}, dimensions={0} | all-to-all | bytes 2097152 | tf_op jit(solution)/shard_map/all_to_all | solution.py:382
  385.9 2.5 backward_heads.1
  388.4 2.2 collective-permute-start.19
  391.6 5.0 %collective-permute-done.19.refs_9_ = bf16[128,768]{1,0:T(8,128)(2,1)S(1)} collective-permute-done((bf16[128,768]{1,0:T(8,128)(2,1)S(1)}, bf16[128,768]{1,0:T(8,128)(2,1)S(1)}, u32[]{:S(2)}, u32[]{:S(2)}) %collective-permute-start.19) | collective-permute-done | bytes 196640 | tf_op jit(solution)/shard_map/ppermute | solution.py:367
  397.7 12.9 %collective-permute-start.20 = (bf16[1024,768]{1,0:T(8,128)(2,1)S(1)}, bf16[1024,768]{1,0:T(8,128)(2,1)S(1)}, u32[]{:S(2)}, u32[]{:S(2)}) collective-permute-start(bf16[1024,768]{1,0:T(8,128)(2,1)S(1)} %weight_grad.4), channel_id=1, source_target_pairs={{0,32},{32,0},{64,96},{96,64},{1,33},{33,1},{65,97},{97,65},{2,34}... | collective-permute-start | bytes 4718600 | tf_op jit(solution)/shard_map/ppermute | solution.py:367
  411.5 4.5 %collective-permute-start.22 = (bf16[512,1024]{1,0:T(8,128)(2,1)S(1)}, bf16[512,1024]{1,0:T(8,128)(2,1)S(1)}, u32[]{:S(2)}, u32[]{:S(2)}) collective-permute-start(bf16[512,1024]{1,0:T(8,128)(2,1)S(1)} %weight_grad.6), channel_id=1, source_target_pairs={{0,32},{32,0},{64,96},{96,64},{1,33},{33,1},{65,97},{97,65},{2,34}... | collective-permute-start | bytes 3145736 | tf_op jit(solution)/shard_map/ppermute | solution.py:367
  416.0 2.3 collective-permute-done.22.refs_8_
  418.3 2.1 weight_grad.7
  420.4 2.8 weight_grad.5
  (134 shorter events, 45.3 us)
Async XLA Ops:
  0.6 15.2 %copy-start = (s32[8]{0:T(128)S(1)}, s32[8]{0:T(128)}, u32[]{:S(2)}) copy-start(s32[8]{0:T(128)} %param.12) | copy-start | bytes 100
  0.6 8.1 %copy-start.8 = (bf16[512,128]{1,0:T(8,128)(2,1)S(1)}, bf16[512,128]{1,0:T(8,128)(2,1)}, u32[]{:S(2)}) copy-start(bf16[512,128]{1,0:T(8,128)(2,1)} %param.19) | copy-start | bytes 393220
  2.6 3.0 collective-permute-start
  5.8 9.9 %copy-start.11 = (s32[8]{0:T(128)S(1)}, s32[8]{0:T(128)}, u32[]{:S(2)}) copy-start(s32[8]{0:T(128)} %param.11) | copy-start | bytes 100
  5.8 11.2 %copy-start.9 = (s32[8,4]{0,1:T(4,128)S(1)}, s32[8,4]{0,1:T(4,128)}, u32[]{:S(2)}) copy-start(s32[8,4]{0,1:T(4,128)} %param.13) | copy-start | bytes 388
  5.9 12.0 %copy-start.10 = (s32[8,4]{0,1:T(4,128)S(1)}, s32[8,4]{0,1:T(4,128)}, u32[]{:S(2)}) copy-start(s32[8,4]{0,1:T(4,128)} %param.14) | copy-start | bytes 388
  5.9 9.1 %collective-permute-start.1 = (bf16[2,128,512]{2,1,0:T(8,128)(2,1)S(1)}, bf16[2,128,512]{2,1,0:T(8,128)(2,1)S(1)}, u32[]{:S(2)}, u32[]{:S(2)}) collective-permute-start(bf16[2,128,512]{2,1,0:T(8,128)(2,1)S(1)} %dynamic-slice_bitcast_fusion), channel_id=1, source_target_pairs={{0,64},{32,96},{64,0},{96,32},{1,65},{33,97},{65,1},{97,33},{2,66}... | collective-permute-start | bytes 786440 | tf_op jit(solution)/shard_map/ppermute | solution.py:367
  9.9 19.1 %all-to-all-start = ((bf16[8,512,128]{2,1,0:T(8,128)(2,1)}), bf16[8,512,128]{2,1,0:T(8,128)(2,1)S(1)}, u32[]{:S(2)}, u32[]{:S(2)}) async-start(bf16[8,512,128]{2,1,0:T(8,128)(2,1)} %broadcast_in_dim.140), calls=%async_computation | async-start | bytes 2097152 | tf_op jit(solution)/shard_map/all_to_all | solution.py:382
  16.4 29.8 %copy-start.6 = (bf16[1,4096,128]{2,1,0:T(8,128)(2,1)S(1)}, bf16[1,4096,128]{2,1,0:T(8,128)(2,1)}, u32[]{:S(2)}) copy-start(bf16[1,4096,128]{2,1,0:T(8,128)(2,1)} %param.16) | copy-start | bytes 3145732
  16.4 29.8 %copy-start.7 = (bf16[1,4096,128]{2,1,0:T(8,128)(2,1)S(1)}, bf16[1,4096,128]{2,1,0:T(8,128)(2,1)}, u32[]{:S(2)}) copy-start(bf16[1,4096,128]{2,1,0:T(8,128)(2,1)} %param.17) | copy-start | bytes 3145732
  46.3 2.2 copy-start.2
  48.4 2.2 copy-start.4
  50.6 38.2 %copy-start.5 = (bf16[1,512,4096]{2,1,0:T(8,128)(2,1)S(1)}, bf16[1,512,4096]{2,1,0:T(8,128)(2,1)}, u32[]{:S(2)}) copy-start(bf16[1,512,4096]{2,1,0:T(8,128)(2,1)} %param.18) | copy-start | bytes 12582916
  69.6 19.3 %copy-start.3 = (bf16[1,4096,512]{2,1,0:T(8,128)(2,1)S(1)}, bf16[1,4096,512]{2,1,0:T(8,128)(2,1)}, u32[]{:S(2)}) copy-start(bf16[1,4096,512]{2,1,0:T(8,128)(2,1)} %param.15) | copy-start | bytes 12582916
  69.6 5.7 %collective-permute-start.2 = (bf16[128,512]{1,0:T(8,128)(2,1)S(1)}, bf16[128,512]{1,0:T(8,128)(2,1)S(1)}, u32[]{:S(2)}, u32[]{:S(2)}) collective-permute-start(bf16[128,512]{1,0:T(8,128)(2,1)S(1)} %add_convert_fusion.7), channel_id=1, source_target_pairs={{0,8},{8,16},{16,24},{1,9},{9,17},{17,25},{2,10},{10,18},{18,26},{... | collective-permute-start | bytes 393224 | tf_op jit(solution)/shard_map/ppermute | solution.py:363
  105.4 5.6 %collective-permute-start.3 = (bf16[128,512]{1,0:T(8,128)(2,1)S(1)}, bf16[128,512]{1,0:T(8,128)(2,1)S(1)}, u32[]{:S(2)}, u32[]{:S(2)}) collective-permute-start(bf16[128,512]{1,0:T(8,128)(2,1)S(1)} %add_convert_fusion.6), channel_id=1, source_target_pairs={{0,8},{8,16},{16,24},{1,9},{9,17},{17,25},{2,10},{10,18},{18,26},{... | collective-permute-start | bytes 393224 | tf_op jit(solution)/shard_map/ppermute | solution.py:363
  139.3 5.7 %collective-permute-start.4 = (bf16[128,512]{1,0:T(8,128)(2,1)S(1)}, bf16[128,512]{1,0:T(8,128)(2,1)S(1)}, u32[]{:S(2)}, u32[]{:S(2)}) collective-permute-start(bf16[128,512]{1,0:T(8,128)(2,1)S(1)} %add_convert_fusion.5), channel_id=1, source_target_pairs={{0,8},{8,16},{16,24},{1,9},{9,17},{17,25},{2,10},{10,18},{18,26},{... | collective-permute-start | bytes 393224 | tf_op jit(solution)/shard_map/ppermute | solution.py:363
  176.8 9.4 %collective-permute-start.6 = (bf16[2,128,512]{2,1,0:T(8,128)(2,1)S(1)}, bf16[2,128,512]{2,1,0:T(8,128)(2,1)S(1)}, u32[]{:S(2)}, u32[]{:S(2)}) collective-permute-start(bf16[2,128,512]{2,1,0:T(8,128)(2,1)S(1)} %select_select_fusion.10), channel_id=1, source_target_pairs={{0,68},{1,69},{2,70},{3,71},{4,64},{5,65},{6,66},{7,67},{32,100},{... | collective-permute-start | bytes 786440 | tf_op jit(solution)/shard_map/ppermute | solution.py:374
  178.5 7.8 %collective-permute-start.7 = (bf16[128,512]{1,0:T(8,128)(2,1)S(1)}, bf16[128,512]{1,0:T(8,128)(2,1)S(1)}, u32[]{:S(2)}, u32[]{:S(2)}) collective-permute-start(bf16[128,512]{1,0:T(8,128)(2,1)S(1)} %select_select_fusion.18), channel_id=1, source_target_pairs={{0,64},{32,96},{64,0},{96,32},{1,65},{33,97},{65,1},{97,33},{2,66}... | collective-permute-start | bytes 393224 | tf_op jit(solution)/shard_map/ppermute | solution.py:367
  179.4 6.9 %collective-permute-start.5 = (bf16[128,512]{1,0:T(8,128)(2,1)S(1)}, bf16[128,512]{1,0:T(8,128)(2,1)S(1)}, u32[]{:S(2)}, u32[]{:S(2)}) collective-permute-start(bf16[128,512]{1,0:T(8,128)(2,1)S(1)} %add_convert_fusion.4), channel_id=1, source_target_pairs={{0,8},{8,16},{16,24},{1,9},{9,17},{17,25},{2,10},{10,18},{18,26},{... | collective-permute-start | bytes 393224 | tf_op jit(solution)/shard_map/ppermute | solution.py:363
  222.7 23.9 %collective-permute-start.9 = (bf16[2,128,512]{2,1,0:T(8,128)(2,1)S(1)}, bf16[2,128,512]{2,1,0:T(8,128)(2,1)S(1)}, u32[]{:S(2)}, u32[]{:S(2)}) collective-permute-start(bf16[2,128,512]{2,1,0:T(8,128)(2,1)S(1)} %select_select_fusion.9), channel_id=1, source_target_pairs={{0,68},{1,69},{2,70},{3,71},{4,64},{5,65},{6,66},{7,67},{32,100},{... | collective-permute-start | bytes 786440 | tf_op jit(solution)/shard_map/ppermute | solution.py:374
  224.3 22.3 %collective-permute-start.10 = (bf16[128,512]{1,0:T(8,128)(2,1)S(1)}, bf16[128,512]{1,0:T(8,128)(2,1)S(1)}, u32[]{:S(2)}, u32[]{:S(2)}) collective-permute-start(bf16[128,512]{1,0:T(8,128)(2,1)S(1)} %select_select_fusion.17), channel_id=1, source_target_pairs={{0,64},{32,96},{64,0},{96,32},{1,65},{33,97},{65,1},{97,33},{2,66}... | collective-permute-start | bytes 393224 | tf_op jit(solution)/shard_map/ppermute | solution.py:367
  225.3 21.3 %collective-permute-start.8 = (bf16[128,512]{1,0:T(8,128)(2,1)S(1)}, bf16[128,512]{1,0:T(8,128)(2,1)S(1)}, u32[]{:S(2)}, u32[]{:S(2)}) collective-permute-start(bf16[128,512]{1,0:T(8,128)(2,1)S(1)} %add_convert_fusion.3), channel_id=1, source_target_pairs={{8,0},{16,8},{24,16},{9,1},{17,9},{25,17},{10,2},{18,10},{26,18},{... | collective-permute-start | bytes 393224 | tf_op jit(solution)/shard_map/ppermute | solution.py:363
  226.6 20.0 %collective-permute-start.11 = (bf16[16,128]{1,0:T(8,128)(2,1)S(1)}, bf16[16,128]{1,0:T(8,128)(2,1)S(1)}, u32[]{:S(2)}, u32[]{:S(2)}) collective-permute-start(bf16[16,128]{1,0:T(8,128)(2,1)S(1)} %slice.70), channel_id=1, source_target_pairs={{0,32},{64,96},{1,33},{65,97},{2,34},{66,98},{3,35},{67,99},{4,36}... | collective-permute-start | bytes 12296 | tf_op jit(solution)/shard_map/ppermute | solution.py:378
  278.9 8.4 %collective-permute-start.13 = (bf16[2,128,512]{2,1,0:T(8,128)(2,1)S(1)}, bf16[2,128,512]{2,1,0:T(8,128)(2,1)S(1)}, u32[]{:S(2)}, u32[]{:S(2)}) collective-permute-start(bf16[2,128,512]{2,1,0:T(8,128)(2,1)S(1)} %select_select_fusion.8), channel_id=1, source_target_pairs={{0,68},{1,69},{2,70},{3,71},{4,64},{5,65},{6,66},{7,67},{32,100},{... | collective-permute-start | bytes 786440 | tf_op jit(solution)/shard_map/ppermute | solution.py:374
  280.6 6.7 %collective-permute-start.12 = (bf16[128,512]{1,0:T(8,128)(2,1)S(1)}, bf16[128,512]{1,0:T(8,128)(2,1)S(1)}, u32[]{:S(2)}, u32[]{:S(2)}) collective-permute-start(bf16[128,512]{1,0:T(8,128)(2,1)S(1)} %add_convert_fusion.2), channel_id=1, source_target_pairs={{8,0},{16,8},{24,16},{9,1},{17,9},{25,17},{10,2},{18,10},{26,18},{... | collective-permute-start | bytes 393224 | tf_op jit(solution)/shard_map/ppermute | solution.py:363
  317.9 10.8 %collective-permute-start.15 = (bf16[2,128,512]{2,1,0:T(8,128)(2,1)S(1)}, bf16[2,128,512]{2,1,0:T(8,128)(2,1)S(1)}, u32[]{:S(2)}, u32[]{:S(2)}) collective-permute-start(bf16[2,128,512]{2,1,0:T(8,128)(2,1)S(1)} %select_select_fusion.7), channel_id=1, source_target_pairs={{0,68},{1,69},{2,70},{3,71},{4,64},{5,65},{6,66},{7,67},{32,100},{... | collective-permute-start | bytes 786440 | tf_op jit(solution)/shard_map/ppermute | solution.py:374
  319.1 9.6 %collective-permute-start.14 = (bf16[128,512]{1,0:T(8,128)(2,1)S(1)}, bf16[128,512]{1,0:T(8,128)(2,1)S(1)}, u32[]{:S(2)}, u32[]{:S(2)}) collective-permute-start(bf16[128,512]{1,0:T(8,128)(2,1)S(1)} %add_convert_fusion.1), channel_id=1, source_target_pairs={{8,0},{16,8},{24,16},{9,1},{17,9},{25,17},{10,2},{18,10},{26,18},{... | collective-permute-start | bytes 393224 | tf_op jit(solution)/shard_map/ppermute | solution.py:363
  359.4 11.7 %collective-permute-start.18 = (bf16[4,128,512]{2,1,0:T(8,128)(2,1)S(1)}, bf16[4,128,512]{2,1,0:T(8,128)(2,1)S(1)}, u32[]{:S(2)}, u32[]{:S(2)}) collective-permute-start(bf16[4,128,512]{2,1,0:T(8,128)(2,1)S(1)} %select_select_fusion.5), channel_id=1, source_target_pairs={{0,68},{1,69},{2,70},{3,71},{4,64},{5,65},{6,66},{7,67},{32,100},{... | collective-permute-start | bytes 1572872 | tf_op jit(solution)/shard_map/ppermute | solution.py:374
  360.9 8.3 %collective-permute-start.17 = (bf16[128,768]{1,0:T(8,128)(2,1)S(1)}, bf16[128,768]{1,0:T(8,128)(2,1)S(1)}, u32[]{:S(2)}, u32[]{:S(2)}) collective-permute-start(bf16[128,768]{1,0:T(8,128)(2,1)S(1)} %select_select_fusion.14), channel_id=1, source_target_pairs={{0,64},{32,96},{64,0},{96,32},{1,65},{33,97},{65,1},{97,33},{2,66}... | collective-permute-start | bytes 589832 | tf_op jit(solution)/shard_map/ppermute | solution.py:367
  361.8 6.3 %collective-permute-start.16 = (bf16[128,512]{1,0:T(8,128)(2,1)S(1)}, bf16[128,512]{1,0:T(8,128)(2,1)S(1)}, u32[]{:S(2)}, u32[]{:S(2)}) collective-permute-start(bf16[128,512]{1,0:T(8,128)(2,1)S(1)} %add_convert_fusion), channel_id=1, source_target_pairs={{8,0},{16,8},{24,16},{9,1},{17,9},{25,17},{10,2},{18,10},{26,18},{... | collective-permute-start | bytes 393224 | tf_op jit(solution)/shard_map/ppermute | solution.py:363
  388.4 8.2 %collective-permute-start.19 = (bf16[128,768]{1,0:T(8,128)(2,1)S(1)}, bf16[128,768]{1,0:T(8,128)(2,1)S(1)}, u32[]{:S(2)}, u32[]{:S(2)}) collective-permute-start(bf16[128,768]{1,0:T(8,128)(2,1)S(1)} %select_select_fusion.11), channel_id=1, source_target_pairs={{0,64},{32,96},{64,0},{96,32},{1,65},{33,97},{65,1},{97,33},{2,66}... | collective-permute-start | bytes 589832 | tf_op jit(solution)/shard_map/ppermute | solution.py:367
  390.7 20.1 %collective-permute-start.21 = (bf16[4,128,512]{2,1,0:T(8,128)(2,1)S(1)}, bf16[4,128,512]{2,1,0:T(8,128)(2,1)S(1)}, u32[]{:S(2)}, u32[]{:S(2)}) collective-permute-start(bf16[4,128,512]{2,1,0:T(8,128)(2,1)S(1)} %select_select_fusion), channel_id=1, source_target_pairs={{0,68},{1,69},{2,70},{3,71},{4,64},{5,65},{6,66},{7,67},{32,100},{... | collective-permute-start | bytes 1572872 | tf_op jit(solution)/shard_map/ppermute | solution.py:374
  397.7 22.7 %collective-permute-start.20 = (bf16[1024,768]{1,0:T(8,128)(2,1)S(1)}, bf16[1024,768]{1,0:T(8,128)(2,1)S(1)}, u32[]{:S(2)}, u32[]{:S(2)}) collective-permute-start(bf16[1024,768]{1,0:T(8,128)(2,1)S(1)} %weight_grad.4), channel_id=1, source_target_pairs={{0,32},{32,0},{64,96},{96,64},{1,33},{33,1},{65,97},{97,65},{2,34}... | collective-permute-start | bytes 4718600 | tf_op jit(solution)/shard_map/ppermute | solution.py:367
  411.5 6.8 %collective-permute-start.22 = (bf16[512,1024]{1,0:T(8,128)(2,1)S(1)}, bf16[512,1024]{1,0:T(8,128)(2,1)S(1)}, u32[]{:S(2)}, u32[]{:S(2)}) collective-permute-start(bf16[512,1024]{1,0:T(8,128)(2,1)S(1)} %weight_grad.6), channel_id=1, source_target_pairs={{0,32},{32,0},{64,96},{96,64},{1,33},{33,1},{65,97},{97,65},{2,34}... | collective-permute-start | bytes 3145736 | tf_op jit(solution)/shard_map/ppermute | solution.py:367
  418.3 4.8 %copy-start.1 = (s32[8]{0:T(128)S(1)}, s32[8]{0:T(128)}, u32[]{:S(2)}) copy-start(s32[8]{0:T(128)} %param.12) | copy-start | bytes 100
where the time goes:
time: 432 us; the launch traced here: 424 us
  blocking collectives  236 us (55%)
  starting transfers between devices  61 us (14%)
  waiting for transfers between devices  54.8 us (13%)
  Pallas kernels  47 us (11%)
  local copies, waits for them, and re-layouts  10.9 us (3%)
  between operations  8.84 us (2%)
  other arithmetic  5.2 us (1%)
    all_to_all x17, blocking collectives, exchange(): lax.all_to_all(blocks, 'tensor', split_axis=0, concat_axis=0, tiled=True)  236 us
    ppermute x8, starting transfers between devices, swapped(): lax.ppermute(x, axis, [(i, i ^ mask) for i in range(lax.axis_size(axis))])  26.8 us
    ppermute x8, waiting for transfers between devices, passed_along(): return lax.ppermute(x, axis, pairs)  24.6 us
    pallas_call x5, Pallas kernels, backward(): pl.pallas_call(functools.partial(backward_kernel, with_input, bool(ends),...  21.9 us
    ppermute x8, starting transfers between devices, passed_along(): return lax.ppermute(x, axis, pairs)  20.4 us
    ppermute x1, waiting for transfers between devices, held_back(): lax.ppermute(x[:16, :128], 'dp', [(i, i + 1) for i in range(0, lax.axis_s...  16 us
    pallas_call x5, Pallas kernels, forward(): pl.pallas_call(functools.partial(forward_kernel, mode, nstep), out_shape=...  12.9 us
    ppermute x8, waiting for transfers between devices, swapped(): lax.ppermute(x, axis, [(i, i ^ mask) for i in range(lax.axis_size(axis))])  10.8 us
  transfers between devices with their start and end apart: 24, of which 14 were waited for; matrix products, arithmetic and copies ran while one was open for 2% of the time, Pallas kernels for 2%

commit v1 on v0

--- a/solution.py
+++ b/solution.py
@@ -298,11 +298,18 @@
     )
 
 
-def weight_grad_kernel(wide_first, runs, nnarrow, splits, quarter_ref, *refs):
+def weight_grad_kernel(wide_first, runs, nnarrow, splits, outs_dtype, quarter_ref, *refs):
     nwide, nout = sum(runs), len(splits)
     wides, narrows = refs[:nwide], refs[nwide : nwide + nnarrow]
-    given, outs = refs[nwide + nnarrow : -nout - 2], refs[-nout - 2 : -2]
-    wide_all, narrow_all = refs[-2:]
+    chunked = outs_dtype == F32
+    if chunked:
+        held, outs = refs[-nout - 3 : -3], refs[-2 * nout - 3 : -nout - 3]
+        wide_all, narrow_all, sems = refs[-3:]
+        given = refs[nwide + nnarrow : -2 * nout - 3]
+    else:
+        given, outs = refs[nwide + nnarrow : -nout - 2], refs[-nout - 2 : -2]
+        wide_all, narrow_all = refs[-2:]
+    saves = []
     quarter = quarter_ref[0]
     at = 0
     for i, n in enumerate(runs):
@@ -332,8 +339,16 @@
             got = dot_tn(narrow_all[:, cols], wide_all[...])
         for more in given:
             got = got + more[cols, :].astype(F32)
-        for out_ref, (start, stop) in zip(outs, splits):
-            out_ref[cols, :] = got[:, start:stop].astype(out_ref.dtype)
+        for i, (start, stop) in enumerate(splits):
+            to = held[i] if chunked else outs[i]
+            to[cols, :] = got[:, start:stop].astype(outs_dtype)
+            if chunked:
+                saves.append(
+                    pltpu.make_async_copy(to.at[cols, :], outs[i].at[cols, :], sems.at[c, i])
+                )
+                saves[-1].start()
+    for save in saves:
+        save.wait()
 
 
 def weight_grad(quarter, wide, narrow, wide_first, widths, dtype, given=()):
@@ -346,11 +361,15 @@
     splits = [(sum(widths[:i]), sum(widths[: i + 1])) for i in range(len(widths))]
     runs = tuple(len(run) for run in wide)
     return pl.pallas_call(
-        functools.partial(weight_grad_kernel, wide_first, runs, len(narrow), tuple(splits)),
+        functools.partial(weight_grad_kernel, wide_first, runs, len(narrow), tuple(splits), dtype),
         out_shape=tuple(jax.ShapeDtypeStruct((height, w), dtype) for w in widths),
         in_specs=[in_smem()] + [in_vmem()] * (len(flat) + len(narrow) + len(given)),
-        out_specs=tuple([in_vmem()] * len(widths)),
-        scratch_shapes=[pltpu.VMEM((total, width), BF16), pltpu.VMEM((total, cols), BF16)],
+        out_specs=tuple([anywhere() if dtype == F32 else in_vmem()] * len(widths)),
+        scratch_shapes=(
+            [pltpu.VMEM((height, w), F32) for w in widths] if dtype == F32 else []
+        )
+        + [pltpu.VMEM((total, width), BF16), pltpu.VMEM((total, cols), BF16)]
+        + ([pltpu.SemaphoreType.DMA((height // 256, len(widths)))] if dtype == F32 else []),
         compiler_params=kernel_params(VMEM_LIMIT),
         cost_estimate=pl.CostEstimate(flops=1, bytes_accessed=1, transcendentals=0),
         name="weight_grad",

time: 432 us -> 431 us (level)
  no operation moved by 1% of the time
where the time goes in v1:
time: 431 us; the launch traced here: 423 us
  blocking collectives  236 us (55%)
  starting transfers between devices  61 us (14%)
  waiting for transfers between devices  54.8 us (13%)
  Pallas kernels  46.1 us (11%)
  local copies, waits for them, and re-layouts  10.9 us (3%)
  between operations  8.89 us (2%)
  other arithmetic  5.2 us (1%)
    all_to_all x17, blocking collectives, exchange(): lax.all_to_all(blocks, 'tensor', split_axis=0, concat_axis=0, tiled=True)  236 us
    ppermute x8, starting transfers between devices, swapped(): lax.ppermute(x, axis, [(i, i ^ mask) for i in range(lax.axis_size(axis))])  26.8 us
    ppermute x8, waiting for transfers between devices, passed_along(): return lax.ppermute(x, axis, pairs)  24.6 us
    pallas_call x5, Pallas kernels, backward(): pl.pallas_call(functools.partial(backward_kernel, with_input, bool(ends),...  21.9 us
    ppermute x8, starting transfers between devices, passed_along(): return lax.ppermute(x, axis, pairs)  20.4 us
    ppermute x1, waiting for transfers between devices, held_back(): lax.ppermute(x[:16, :128], 'dp', [(i, i + 1) for i in range(0, lax.axis_s...  16 us
    pallas_call x5, Pallas kernels, forward(): pl.pallas_call(functools.partial(forward_kernel, mode, nstep), out_shape=...  12.9 us
    ppermute x8, waiting for transfers between devices, swapped(): lax.ppermute(x, axis, [(i, i ^ mask) for i in range(lax.axis_size(axis))])  10.8 us
  transfers between devices with their start and end apart: 24, of which 14 were waited for; matrix products, arithmetic and copies ran while one was open for 2% of the time, Pallas kernels for 2%

profile of v1, /device:TPU:1, one launch (start us, length us, event | category | flops | bytes accessed | tf_op | source)
XLA Modules:
  0.0 422.8 jit_solution(11533277255798480190)
XLA Ops:
  5.9 2.9 collective-permute-start.1
  9.9 4.2 all-to-all-start
  29.1 17.1 %all_to_all.90.x_ref = bf16[8,128,512]{2,1,0:T(8,128)(2,1)S(1)} all-to-all(bf16[8,128,512]{2,1,0:T(8,128)(2,1)S(1)} %broadcast_in_dim.141), channel_id=1, replica_groups=mesh['dp'=4,'section'=4,'tensor'=8] {'tensor'}, dimensions={0} | all-to-all | bytes 2097152 | tf_op jit(solution)/shard_map/all_to_all | solution.py:401
  46.3 2.2 copy-done.2
  48.4 2.2 copy-done.4
  50.6 2.5 forward_layer.5
  53.2 16.2 %all_to_all.91 = bf16[8,128,512]{2,1,0:T(8,128)(2,1)S(1)} all-to-all(bf16[8,128,512]{2,1,0:T(8,128)(2,1)S(1)} %get-tuple-element.173), channel_id=1, replica_groups=mesh['dp'=4,'section'=4,'tensor'=8] {'tensor'}, dimensions={0} | all-to-all | bytes 2097152 | tf_op jit(solution)/shard_map/all_to_all | solution.py:401
  69.6 3.8 collective-permute-start.2
  73.5 1.9 collective-permute-done.2
  75.5 13.4 %all_to_all.92.x_ref = bf16[8,128,512]{2,1,0:T(8,128)(2,1)S(1)} all-to-all(bf16[8,128,512]{2,1,0:T(8,128)(2,1)S(1)} %broadcast_in_dim.142), channel_id=1, replica_groups=mesh['dp'=4,'section'=4,'tensor'=8] {'tensor'}, dimensions={0} | all-to-all | bytes 2097152 | tf_op jit(solution)/shard_map/all_to_all | solution.py:401
  88.9 2.5 forward_layer.6
  91.4 13.8 %all_to_all.93 = bf16[8,128,512]{2,1,0:T(8,128)(2,1)S(1)} all-to-all(bf16[8,128,512]{2,1,0:T(8,128)(2,1)S(1)} %get-tuple-element.177), channel_id=1, replica_groups=mesh['dp'=4,'section'=4,'tensor'=8] {'tensor'}, dimensions={0} | all-to-all | bytes 2097152 | tf_op jit(solution)/shard_map/all_to_all | solution.py:401
  105.4 3.6 collective-permute-start.3
  111.1 12.7 %all_to_all.94.x_ref = bf16[8,128,512]{2,1,0:T(8,128)(2,1)S(1)} all-to-all(bf16[8,128,512]{2,1,0:T(8,128)(2,1)S(1)} %broadcast_in_dim.143), channel_id=1, replica_groups=mesh['dp'=4,'section'=4,'tensor'=8] {'tensor'}, dimensions={0} | all-to-all | bytes 2097152 | tf_op jit(solution)/shard_map/all_to_all | solution.py:401
  123.8 2.5 forward_layer.7
  126.4 12.7 %all_to_all.95 = bf16[8,128,512]{2,1,0:T(8,128)(2,1)S(1)} all-to-all(bf16[8,128,512]{2,1,0:T(8,128)(2,1)S(1)} %get-tuple-element.183), channel_id=1, replica_groups=mesh['dp'=4,'section'=4,'tensor'=8] {'tensor'}, dimensions={0} | all-to-all | bytes 2097152 | tf_op jit(solution)/shard_map/all_to_all | solution.py:401
  139.3 3.8 collective-permute-start.4
  145.1 12.9 %all_to_all.96.x_ref = bf16[8,128,512]{2,1,0:T(8,128)(2,1)S(1)} all-to-all(bf16[8,128,512]{2,1,0:T(8,128)(2,1)S(1)} %broadcast_in_dim.144), channel_id=1, replica_groups=mesh['dp'=4,'section'=4,'tensor'=8] {'tensor'}, dimensions={0} | all-to-all | bytes 2097152 | tf_op jit(solution)/shard_map/all_to_all | solution.py:401
  158.0 2.7 forward_layer.8
  160.7 15.9 %all_to_all.97.got_ref = bf16[8,160,512]{2,1,0:T(8,128)(2,1)S(1)} all-to-all(bf16[8,160,512]{2,1,0:T(8,128)(2,1)S(1)} %get-tuple-element.188), channel_id=1, replica_groups=mesh['dp'=4,'section'=4,'tensor'=8] {'tensor'}, dimensions={0} | all-to-all | bytes 2621440 | tf_op jit(solution)/shard_map/all_to_all | solution.py:401
  179.4 4.1 collective-permute-start.5
  183.5 2.7 step_end_grad.2.g_ref
  186.4 14.0 %all_to_all.98.x_ref = bf16[8,128,512]{2,1,0:T(8,128)(2,1)S(1)} all-to-all(bf16[8,128,512]{2,1,0:T(8,128)(2,1)S(1)} %broadcast_in_dim.145), channel_id=1, replica_groups=mesh['dp'=4,'section'=4,'tensor'=8] {'tensor'}, dimensions={0} | all-to-all | bytes 2097152 | tf_op jit(solution)/shard_map/all_to_all | solution.py:401
  200.4 2.6 forward_layer.9
  203.0 4.8 %backward_layer.4 = (bf16[128,768]{1,0:T(8,128)(2,1)S(1)}, bf16[8,160,512]{2,1,0:T(8,128)(2,1)S(1)}) custom-call(s32[1]{0:T(128)} %constant.63.clone.1.flag_ref, bf16[8,128,512]{2,1,0:T(8,128)(2,1)S(1)} %step_end_grad.2.g_ref, bf16[1280,128]{1,0:T(8,128)(2,1)S(1)} %get-tuple-element.210.pack0_ref.pack1_ref, ...), custom_call_target="tpu_custom_call" | custom-call | flops 1342177280 | bytes 10485760 | tf_op jit(solution)/shard_map/backward_layer/pallas_call | solution.py:278
  207.8 14.6 %all_to_all.99.got_ref = bf16[8,160,512]{2,1,0:T(8,128)(2,1)S(1)} all-to-all(bf16[8,160,512]{2,1,0:T(8,128)(2,1)S(1)} %get-tuple-element.216), channel_id=1, replica_groups=mesh['dp'=4,'section'=4,'tensor'=8] {'tensor'}, dimensions={0} | all-to-all | bytes 2621440 | tf_op jit(solution)/shard_map/all_to_all | solution.py:401
  227.9 2.7 step_end_grad.3
  230.6 16.0 %collective-permute-done.11.rest_0_ = bf16[16,128]{1,0:T(8,128)(2,1)S(1)} collective-permute-done((bf16[16,128]{1,0:T(8,128)(2,1)S(1)}, bf16[16,128]{1,0:T(8,128)(2,1)S(1)}, u32[]{:S(2)}, u32[]{:S(2)}) %collective-permute-start.11) | collective-permute-done | bytes 4128 | tf_op jit(solution)/shard_map/ppermute | solution.py:397
  246.7 13.4 %all_to_all.100.g_ref = bf16[8,128,512]{2,1,0:T(8,128)(2,1)S(1)} all-to-all(bf16[8,128,512]{2,1,0:T(8,128)(2,1)S(1)} %broadcast_in_dim.146), channel_id=1, replica_groups=mesh['dp'=4,'section'=4,'tensor'=8] {'tensor'}, dimensions={0} | all-to-all | bytes 2097152 | tf_op jit(solution)/shard_map/all_to_all | solution.py:401
  260.2 5.0 %backward_layer.5 = (bf16[128,768]{1,0:T(8,128)(2,1)S(1)}, bf16[8,128,512]{2,1,0:T(8,128)(2,1)S(1)}) custom-call(s32[1]{0:T(128)} %bitcast.20.flag_ref, bf16[8,128,512]{2,1,0:T(8,128)(2,1)S(1)} %all_to_all.100.g_ref, bf16[1280,128]{1,0:T(8,128)(2,1)S(1)} %get-tuple-element.233.pack0_ref.pack1_ref, bf16[1280,128]{1,0:T(8,128)(2,1)S(1)} %get-tuple-element.234.pack1_ref, ...), custom_call_target="tpu_custom_call" | custom-call | flops 1342177280 | bytes 10485760 | tf_op jit(solution)/shard_map/backward_layer/pallas_call | solution.py:278
  265.2 13.5 %all_to_all.101 = bf16[8,128,512]{2,1,0:T(8,128)(2,1)S(1)} all-to-all(bf16[8,128,512]{2,1,0:T(8,128)(2,1)S(1)} %get-tuple-element.239), channel_id=1, replica_groups=mesh['dp'=4,'section'=4,'tensor'=8] {'tensor'}, dimensions={0} | all-to-all | bytes 2097152 | tf_op jit(solution)/shard_map/all_to_all | solution.py:401
  281.9 5.4 %collective-permute-done.12 = bf16[128,512]{1,0:T(8,128)(2,1)S(1)} collective-permute-done((bf16[128,512]{1,0:T(8,128)(2,1)S(1)}, bf16[128,512]{1,0:T(8,128)(2,1)S(1)}, u32[]{:S(2)}, u32[]{:S(2)}) %collective-permute-start.12) | collective-permute-done | bytes 131104 | tf_op jit(solution)/shard_map/ppermute | solution.py:382
  287.4 12.7 %all_to_all.102.g_ref = bf16[8,128,512]{2,1,0:T(8,128)(2,1)S(1)} all-to-all(bf16[8,128,512]{2,1,0:T(8,128)(2,1)S(1)} %broadcast_in_dim.147), channel_id=1, replica_groups=mesh['dp'=4,'section'=4,'tensor'=8] {'tensor'}, dimensions={0} | all-to-all | bytes 2097152 | tf_op jit(solution)/shard_map/all_to_all | solution.py:401
  300.2 4.8 %backward_layer.6 = (bf16[128,768]{1,0:T(8,128)(2,1)S(1)}, bf16[8,128,512]{2,1,0:T(8,128)(2,1)S(1)}) custom-call(s32[1]{0:T(128)} %bitcast.19.flag_ref, bf16[8,128,512]{2,1,0:T(8,128)(2,1)S(1)} %all_to_all.102.g_ref, bf16[1280,128]{1,0:T(8,128)(2,1)S(1)} %get-tuple-element.250.pack0_ref.pack1_ref, ...), custom_call_target="tpu_custom_call" | custom-call | flops 1342177280 | bytes 10485760 | tf_op jit(solution)/shard_map/backward_layer/pallas_call | solution.py:278
  305.0 12.7 %all_to_all.103 = bf16[8,128,512]{2,1,0:T(8,128)(2,1)S(1)} all-to-all(bf16[8,128,512]{2,1,0:T(8,128)(2,1)S(1)} %get-tuple-element.252), channel_id=1, replica_groups=mesh['dp'=4,'section'=4,'tensor'=8] {'tensor'}, dimensions={0} | all-to-all | bytes 2097152 | tf_op jit(solution)/shard_map/all_to_all | solution.py:401
  320.4 8.3 %collective-permute-done.14 = bf16[128,512]{1,0:T(8,128)(2,1)S(1)} collective-permute-done((bf16[128,512]{1,0:T(8,128)(2,1)S(1)}, bf16[128,512]{1,0:T(8,128)(2,1)S(1)}, u32[]{:S(2)}, u32[]{:S(2)}) %collective-permute-start.14) | collective-permute-done | bytes 131104 | tf_op jit(solution)/shard_map/ppermute | solution.py:382
  328.8 12.7 %all_to_all.104.g_ref = bf16[8,128,512]{2,1,0:T(8,128)(2,1)S(1)} all-to-all(bf16[8,128,512]{2,1,0:T(8,128)(2,1)S(1)} %broadcast_in_dim.148), channel_id=1, replica_groups=mesh['dp'=4,'section'=4,'tensor'=8] {'tensor'}, dimensions={0} | all-to-all | bytes 2097152 | tf_op jit(solution)/shard_map/all_to_all | solution.py:401
  341.5 4.8 %backward_layer.7 = (bf16[128,768]{1,0:T(8,128)(2,1)S(1)}, bf16[8,128,512]{2,1,0:T(8,128)(2,1)S(1)}) custom-call(s32[1]{0:T(128)} %bitcast.18.flag_ref, bf16[8,128,512]{2,1,0:T(8,128)(2,1)S(1)} %all_to_all.104.g_ref, bf16[1280,128]{1,0:T(8,128)(2,1)S(1)} %get-tuple-element.264.pack0_ref, bf16[1280,128]{1,0:T(8,128)(2,1)S(1)} %get-tuple-element.233.pack0_ref.pack1_ref, ...), custom_call_target="tpu_custom_call" | custom-call | flops 1342177280 | bytes 10485760 | tf_op jit(solution)/shard_map/backward_layer/pallas_call | solution.py:278
  346.3 12.7 %all_to_all.105 = bf16[8,128,512]{2,1,0:T(8,128)(2,1)S(1)} all-to-all(bf16[8,128,512]{2,1,0:T(8,128)(2,1)S(1)} %get-tuple-element.266), channel_id=1, replica_groups=mesh['dp'=4,'section'=4,'tensor'=8] {'tensor'}, dimensions={0} | all-to-all | bytes 2097152 | tf_op jit(solution)/shard_map/all_to_all | solution.py:401
  363.1 5.0 %collective-permute-done.16 = bf16[128,512]{1,0:T(8,128)(2,1)S(1)} collective-permute-done((bf16[128,512]{1,0:T(8,128)(2,1)S(1)}, bf16[128,512]{1,0:T(8,128)(2,1)S(1)}, u32[]{:S(2)}, u32[]{:S(2)}) %collective-permute-start.16) | collective-permute-done | bytes 131104 | tf_op jit(solution)/shard_map/ppermute | solution.py:382
  371.2 14.7 %all_to_all.106.g_ref = bf16[8,128,512]{2,1,0:T(8,128)(2,1)S(1)} all-to-all(bf16[8,128,512]{2,1,0:T(8,128)(2,1)S(1)} %broadcast_in_dim.149), channel_id=1, replica_groups=mesh['dp'=4,'section'=4,'tensor'=8] {'tensor'}, dimensions={0} | all-to-all | bytes 2097152 | tf_op jit(solution)/shard_map/all_to_all | solution.py:401
  385.9 2.5 backward_heads.1
  388.4 2.2 collective-permute-start.19
  391.6 5.0 %collective-permute-done.19.refs_9_ = bf16[128,768]{1,0:T(8,128)(2,1)S(1)} collective-permute-done((bf16[128,768]{1,0:T(8,128)(2,1)S(1)}, bf16[128,768]{1,0:T(8,128)(2,1)S(1)}, u32[]{:S(2)}, u32[]{:S(2)}) %collective-permute-start.19) | collective-permute-done | bytes 196640 | tf_op jit(solution)/shard_map/ppermute | solution.py:386
  397.7 12.9 %collective-permute-start.20 = (bf16[1024,768]{1,0:T(8,128)(2,1)S(1)}, bf16[1024,768]{1,0:T(8,128)(2,1)S(1)}, u32[]{:S(2)}, u32[]{:S(2)}) collective-permute-start(bf16[1024,768]{1,0:T(8,128)(2,1)S(1)} %weight_grad.4), channel_id=1, source_target_pairs={{0,32},{32,0},{64,96},{96,64},{1,33},{33,1},{65,97},{97,65},{2,34}... | collective-permute-start | bytes 4718600 | tf_op jit(solution)/shard_map/ppermute | solution.py:386
  411.5 4.5 %collective-permute-start.22 = (bf16[512,1024]{1,0:T(8,128)(2,1)S(1)}, bf16[512,1024]{1,0:T(8,128)(2,1)S(1)}, u32[]{:S(2)}, u32[]{:S(2)}) collective-permute-start(bf16[512,1024]{1,0:T(8,128)(2,1)S(1)} %weight_grad.6), channel_id=1, source_target_pairs={{0,32},{32,0},{64,96},{96,64},{1,33},{33,1},{65,97},{97,65},{2,34}... | collective-permute-start | bytes 3145736 | tf_op jit(solution)/shard_map/ppermute | solution.py:386
  416.0 2.3 collective-permute-done.22.refs_8_
  420.1 2.2 weight_grad.5
  (134 shorter events, 45.1 us)
Async XLA Ops:
  0.6 15.2 %copy-start = (s32[8]{0:T(128)S(1)}, s32[8]{0:T(128)}, u32[]{:S(2)}) copy-start(s32[8]{0:T(128)} %param.12) | copy-start | bytes 100
  0.6 8.1 %copy-start.8 = (bf16[512,128]{1,0:T(8,128)(2,1)S(1)}, bf16[512,128]{1,0:T(8,128)(2,1)}, u32[]{:S(2)}) copy-start(bf16[512,128]{1,0:T(8,128)(2,1)} %param.19) | copy-start | bytes 393220
  2.6 3.0 collective-permute-start
  5.8 9.9 %copy-start.11 = (s32[8]{0:T(128)S(1)}, s32[8]{0:T(128)}, u32[]{:S(2)}) copy-start(s32[8]{0:T(128)} %param.11) | copy-start | bytes 100
  5.8 11.2 %copy-start.9 = (s32[8,4]{0,1:T(4,128)S(1)}, s32[8,4]{0,1:T(4,128)}, u32[]{:S(2)}) copy-start(s32[8,4]{0,1:T(4,128)} %param.13) | copy-start | bytes 388
  5.9 12.0 %copy-start.10 = (s32[8,4]{0,1:T(4,128)S(1)}, s32[8,4]{0,1:T(4,128)}, u32[]{:S(2)}) copy-start(s32[8,4]{0,1:T(4,128)} %param.14) | copy-start | bytes 388
  5.9 9.1 %collective-permute-start.1 = (bf16[2,128,512]{2,1,0:T(8,128)(2,1)S(1)}, bf16[2,128,512]{2,1,0:T(8,128)(2,1)S(1)}, u32[]{:S(2)}, u32[]{:S(2)}) collective-permute-start(bf16[2,128,512]{2,1,0:T(8,128)(2,1)S(1)} %dynamic-slice_bitcast_fusion), channel_id=1, source_target_pairs={{0,64},{32,96},{64,0},{96,32},{1,65},{33,97},{65,1},{97,33},{2,66}... | collective-permute-start | bytes 786440 | tf_op jit(solution)/shard_map/ppermute | solution.py:386
  9.9 19.1 %all-to-all-start = ((bf16[8,512,128]{2,1,0:T(8,128)(2,1)}), bf16[8,512,128]{2,1,0:T(8,128)(2,1)S(1)}, u32[]{:S(2)}, u32[]{:S(2)}) async-start(bf16[8,512,128]{2,1,0:T(8,128)(2,1)} %broadcast_in_dim.140), calls=%async_computation | async-start | bytes 2097152 | tf_op jit(solution)/shard_map/all_to_all | solution.py:401
  16.4 29.8 %copy-start.6 = (bf16[1,4096,128]{2,1,0:T(8,128)(2,1)S(1)}, bf16[1,4096,128]{2,1,0:T(8,128)(2,1)}, u32[]{:S(2)}) copy-start(bf16[1,4096,128]{2,1,0:T(8,128)(2,1)} %param.16) | copy-start | bytes 3145732
  16.4 29.8 %copy-start.7 = (bf16[1,4096,128]{2,1,0:T(8,128)(2,1)S(1)}, bf16[1,4096,128]{2,1,0:T(8,128)(2,1)}, u32[]{:S(2)}) copy-start(bf16[1,4096,128]{2,1,0:T(8,128)(2,1)} %param.17) | copy-start | bytes 3145732
  46.3 2.2 copy-start.2
  48.4 2.2 copy-start.4
  50.6 38.2 %copy-start.5 = (bf16[1,512,4096]{2,1,0:T(8,128)(2,1)S(1)}, bf16[1,512,4096]{2,1,0:T(8,128)(2,1)}, u32[]{:S(2)}) copy-start(bf16[1,512,4096]{2,1,0:T(8,128)(2,1)} %param.18) | copy-start | bytes 12582916
  69.6 19.3 %copy-start.3 = (bf16[1,4096,512]{2,1,0:T(8,128)(2,1)S(1)}, bf16[1,4096,512]{2,1,0:T(8,128)(2,1)}, u32[]{:S(2)}) copy-start(bf16[1,4096,512]{2,1,0:T(8,128)(2,1)} %param.15) | copy-start | bytes 12582916
  69.6 5.7 %collective-permute-start.2 = (bf16[128,512]{1,0:T(8,128)(2,1)S(1)}, bf16[128,512]{1,0:T(8,128)(2,1)S(1)}, u32[]{:S(2)}, u32[]{:S(2)}) collective-permute-start(bf16[128,512]{1,0:T(8,128)(2,1)S(1)} %add_convert_fusion.7), channel_id=1, source_target_pairs={{0,8},{8,16},{16,24},{1,9},{9,17},{17,25},{2,10},{10,18},{18,26},{... | collective-permute-start | bytes 393224 | tf_op jit(solution)/shard_map/ppermute | solution.py:382
  105.4 5.6 %collective-permute-start.3 = (bf16[128,512]{1,0:T(8,128)(2,1)S(1)}, bf16[128,512]{1,0:T(8,128)(2,1)S(1)}, u32[]{:S(2)}, u32[]{:S(2)}) collective-permute-start(bf16[128,512]{1,0:T(8,128)(2,1)S(1)} %add_convert_fusion.6), channel_id=1, source_target_pairs={{0,8},{8,16},{16,24},{1,9},{9,17},{17,25},{2,10},{10,18},{18,26},{... | collective-permute-start | bytes 393224 | tf_op jit(solution)/shard_map/ppermute | solution.py:382
  139.3 5.7 %collective-permute-start.4 = (bf16[128,512]{1,0:T(8,128)(2,1)S(1)}, bf16[128,512]{1,0:T(8,128)(2,1)S(1)}, u32[]{:S(2)}, u32[]{:S(2)}) collective-permute-start(bf16[128,512]{1,0:T(8,128)(2,1)S(1)} %add_convert_fusion.5), channel_id=1, source_target_pairs={{0,8},{8,16},{16,24},{1,9},{9,17},{17,25},{2,10},{10,18},{18,26},{... | collective-permute-start | bytes 393224 | tf_op jit(solution)/shard_map/ppermute | solution.py:382
  176.8 9.4 %collective-permute-start.6 = (bf16[2,128,512]{2,1,0:T(8,128)(2,1)S(1)}, bf16[2,128,512]{2,1,0:T(8,128)(2,1)S(1)}, u32[]{:S(2)}, u32[]{:S(2)}) collective-permute-start(bf16[2,128,512]{2,1,0:T(8,128)(2,1)S(1)} %select_select_fusion.10), channel_id=1, source_target_pairs={{0,68},{1,69},{2,70},{3,71},{4,64},{5,65},{6,66},{7,67},{32,100},{... | collective-permute-start | bytes 786440 | tf_op jit(solution)/shard_map/ppermute | solution.py:393
  178.5 7.8 %collective-permute-start.7 = (bf16[128,512]{1,0:T(8,128)(2,1)S(1)}, bf16[128,512]{1,0:T(8,128)(2,1)S(1)}, u32[]{:S(2)}, u32[]{:S(2)}) collective-permute-start(bf16[128,512]{1,0:T(8,128)(2,1)S(1)} %select_select_fusion.18), channel_id=1, source_target_pairs={{0,64},{32,96},{64,0},{96,32},{1,65},{33,97},{65,1},{97,33},{2,66}... | collective-permute-start | bytes 393224 | tf_op jit(solution)/shard_map/ppermute | solution.py:386
  179.4 6.9 %collective-permute-start.5 = (bf16[128,512]{1,0:T(8,128)(2,1)S(1)}, bf16[128,512]{1,0:T(8,128)(2,1)S(1)}, u32[]{:S(2)}, u32[]{:S(2)}) collective-permute-start(bf16[128,512]{1,0:T(8,128)(2,1)S(1)} %add_convert_fusion.4), channel_id=1, source_target_pairs={{0,8},{8,16},{16,24},{1,9},{9,17},{17,25},{2,10},{10,18},{18,26},{... | collective-permute-start | bytes 393224 | tf_op jit(solution)/shard_map/ppermute | solution.py:382
  222.7 23.9 %collective-permute-start.9 = (bf16[2,128,512]{2,1,0:T(8,128)(2,1)S(1)}, bf16[2,128,512]{2,1,0:T(8,128)(2,1)S(1)}, u32[]{:S(2)}, u32[]{:S(2)}) collective-permute-start(bf16[2,128,512]{2,1,0:T(8,128)(2,1)S(1)} %select_select_fusion.9), channel_id=1, source_target_pairs={{0,68},{1,69},{2,70},{3,71},{4,64},{5,65},{6,66},{7,67},{32,100},{... | collective-permute-start | bytes 786440 | tf_op jit(solution)/shard_map/ppermute | solution.py:393
  224.3 22.3 %collective-permute-start.10 = (bf16[128,512]{1,0:T(8,128)(2,1)S(1)}, bf16[128,512]{1,0:T(8,128)(2,1)S(1)}, u32[]{:S(2)}, u32[]{:S(2)}) collective-permute-start(bf16[128,512]{1,0:T(8,128)(2,1)S(1)} %select_select_fusion.17), channel_id=1, source_target_pairs={{0,64},{32,96},{64,0},{96,32},{1,65},{33,97},{65,1},{97,33},{2,66}... | collective-permute-start | bytes 393224 | tf_op jit(solution)/shard_map/ppermute | solution.py:386
  225.3 21.3 %collective-permute-start.8 = (bf16[128,512]{1,0:T(8,128)(2,1)S(1)}, bf16[128,512]{1,0:T(8,128)(2,1)S(1)}, u32[]{:S(2)}, u32[]{:S(2)}) collective-permute-start(bf16[128,512]{1,0:T(8,128)(2,1)S(1)} %add_convert_fusion.3), channel_id=1, source_target_pairs={{8,0},{16,8},{24,16},{9,1},{17,9},{25,17},{10,2},{18,10},{26,18},{... | collective-permute-start | bytes 393224 | tf_op jit(solution)/shard_map/ppermute | solution.py:382
  226.6 20.0 %collective-permute-start.11 = (bf16[16,128]{1,0:T(8,128)(2,1)S(1)}, bf16[16,128]{1,0:T(8,128)(2,1)S(1)}, u32[]{:S(2)}, u32[]{:S(2)}) collective-permute-start(bf16[16,128]{1,0:T(8,128)(2,1)S(1)} %slice.70), channel_id=1, source_target_pairs={{0,32},{64,96},{1,33},{65,97},{2,34},{66,98},{3,35},{67,99},{4,36}... | collective-permute-start | bytes 12296 | tf_op jit(solution)/shard_map/ppermute | solution.py:397
  278.9 8.4 %collective-permute-start.13 = (bf16[2,128,512]{2,1,0:T(8,128)(2,1)S(1)}, bf16[2,128,512]{2,1,0:T(8,128)(2,1)S(1)}, u32[]{:S(2)}, u32[]{:S(2)}) collective-permute-start(bf16[2,128,512]{2,1,0:T(8,128)(2,1)S(1)} %select_select_fusion.8), channel_id=1, source_target_pairs={{0,68},{1,69},{2,70},{3,71},{4,64},{5,65},{6,66},{7,67},{32,100},{... | collective-permute-start | bytes 786440 | tf_op jit(solution)/shard_map/ppermute | solution.py:393
  280.6 6.7 %collective-permute-start.12 = (bf16[128,512]{1,0:T(8,128)(2,1)S(1)}, bf16[128,512]{1,0:T(8,128)(2,1)S(1)}, u32[]{:S(2)}, u32[]{:S(2)}) collective-permute-start(bf16[128,512]{1,0:T(8,128)(2,1)S(1)} %add_convert_fusion.2), channel_id=1, source_target_pairs={{8,0},{16,8},{24,16},{9,1},{17,9},{25,17},{10,2},{18,10},{26,18},{... | collective-permute-start | bytes 393224 | tf_op jit(solution)/shard_map/ppermute | solution.py:382
  317.9 10.8 %collective-permute-start.15 = (bf16[2,128,512]{2,1,0:T(8,128)(2,1)S(1)}, bf16[2,128,512]{2,1,0:T(8,128)(2,1)S(1)}, u32[]{:S(2)}, u32[]{:S(2)}) collective-permute-start(bf16[2,128,512]{2,1,0:T(8,128)(2,1)S(1)} %select_select_fusion.7), channel_id=1, source_target_pairs={{0,68},{1,69},{2,70},{3,71},{4,64},{5,65},{6,66},{7,67},{32,100},{... | collective-permute-start | bytes 786440 | tf_op jit(solution)/shard_map/ppermute | solution.py:393
  319.1 9.6 %collective-permute-start.14 = (bf16[128,512]{1,0:T(8,128)(2,1)S(1)}, bf16[128,512]{1,0:T(8,128)(2,1)S(1)}, u32[]{:S(2)}, u32[]{:S(2)}) collective-permute-start(bf16[128,512]{1,0:T(8,128)(2,1)S(1)} %add_convert_fusion.1), channel_id=1, source_target_pairs={{8,0},{16,8},{24,16},{9,1},{17,9},{25,17},{10,2},{18,10},{26,18},{... | collective-permute-start | bytes 393224 | tf_op jit(solution)/shard_map/ppermute | solution.py:382
  359.4 11.7 %collective-permute-start.18 = (bf16[4,128,512]{2,1,0:T(8,128)(2,1)S(1)}, bf16[4,128,512]{2,1,0:T(8,128)(2,1)S(1)}, u32[]{:S(2)}, u32[]{:S(2)}) collective-permute-start(bf16[4,128,512]{2,1,0:T(8,128)(2,1)S(1)} %select_select_fusion.5), channel_id=1, source_target_pairs={{0,68},{1,69},{2,70},{3,71},{4,64},{5,65},{6,66},{7,67},{32,100},{... | collective-permute-start | bytes 1572872 | tf_op jit(solution)/shard_map/ppermute | solution.py:393
  360.9 8.3 %collective-permute-start.17 = (bf16[128,768]{1,0:T(8,128)(2,1)S(1)}, bf16[128,768]{1,0:T(8,128)(2,1)S(1)}, u32[]{:S(2)}, u32[]{:S(2)}) collective-permute-start(bf16[128,768]{1,0:T(8,128)(2,1)S(1)} %select_select_fusion.14), channel_id=1, source_target_pairs={{0,64},{32,96},{64,0},{96,32},{1,65},{33,97},{65,1},{97,33},{2,66}... | collective-permute-start | bytes 589832 | tf_op jit(solution)/shard_map/ppermute | solution.py:386
  361.8 6.3 %collective-permute-start.16 = (bf16[128,512]{1,0:T(8,128)(2,1)S(1)}, bf16[128,512]{1,0:T(8,128)(2,1)S(1)}, u32[]{:S(2)}, u32[]{:S(2)}) collective-permute-start(bf16[128,512]{1,0:T(8,128)(2,1)S(1)} %add_convert_fusion), channel_id=1, source_target_pairs={{8,0},{16,8},{24,16},{9,1},{17,9},{25,17},{10,2},{18,10},{26,18},{... | collective-permute-start | bytes 393224 | tf_op jit(solution)/shard_map/ppermute | solution.py:382
  388.4 8.2 %collective-permute-start.19 = (bf16[128,768]{1,0:T(8,128)(2,1)S(1)}, bf16[128,768]{1,0:T(8,128)(2,1)S(1)}, u32[]{:S(2)}, u32[]{:S(2)}) collective-permute-start(bf16[128,768]{1,0:T(8,128)(2,1)S(1)} %select_select_fusion.11), channel_id=1, source_target_pairs={{0,64},{32,96},{64,0},{96,32},{1,65},{33,97},{65,1},{97,33},{2,66}... | collective-permute-start | bytes 589832 | tf_op jit(solution)/shard_map/ppermute | solution.py:386
  390.7 20.1 %collective-permute-start.21 = (bf16[4,128,512]{2,1,0:T(8,128)(2,1)S(1)}, bf16[4,128,512]{2,1,0:T(8,128)(2,1)S(1)}, u32[]{:S(2)}, u32[]{:S(2)}) collective-permute-start(bf16[4,128,512]{2,1,0:T(8,128)(2,1)S(1)} %select_select_fusion), channel_id=1, source_target_pairs={{0,68},{1,69},{2,70},{3,71},{4,64},{5,65},{6,66},{7,67},{32,100},{... | collective-permute-start | bytes 1572872 | tf_op jit(solution)/shard_map/ppermute | solution.py:393
  397.7 22.4 %collective-permute-start.20 = (bf16[1024,768]{1,0:T(8,128)(2,1)S(1)}, bf16[1024,768]{1,0:T(8,128)(2,1)S(1)}, u32[]{:S(2)}, u32[]{:S(2)}) collective-permute-start(bf16[1024,768]{1,0:T(8,128)(2,1)S(1)} %weight_grad.4), channel_id=1, source_target_pairs={{0,32},{32,0},{64,96},{96,64},{1,33},{33,1},{65,97},{97,65},{2,34}... | collective-permute-start | bytes 4718600 | tf_op jit(solution)/shard_map/ppermute | solution.py:386
  411.5 6.8 %collective-permute-start.22 = (bf16[512,1024]{1,0:T(8,128)(2,1)S(1)}, bf16[512,1024]{1,0:T(8,128)(2,1)S(1)}, u32[]{:S(2)}, u32[]{:S(2)}) collective-permute-start(bf16[512,1024]{1,0:T(8,128)(2,1)S(1)} %weight_grad.6), channel_id=1, source_target_pairs={{0,32},{32,0},{64,96},{96,64},{1,33},{33,1},{65,97},{97,65},{2,34}... | collective-permute-start | bytes 3145736 | tf_op jit(solution)/shard_map/ppermute | solution.py:386
  418.3 4.0 copy-start.1
